TPU v7x, 32 devices: a whole 2x2x4 slice. The times are simulated.
32 devices in a mesh: rep: 4 (over y, x), fsdp: 8 (over z, core).
Axes of the slice: x: 2, y: 2, z: 4, core: 2. Of those that a mesh axis runs over, the one named last changes fastest.
Arguments:
- block_input: bfloat16 [32768, 768], P(('rep', 'fsdp')), may hold values from -6 to 6
- cotangent: bfloat16 [32768, 768], P(('rep', 'fsdp')), may hold values from -6 to 6
- lengths: int32 [32], P(('rep', 'fsdp')), may hold values from 128 to 1024, as said below
- first_gain: bfloat16 [768], P('fsdp'), may hold values from 0.5 to 1.5
- first_shift: bfloat16 [768], P('fsdp'), may hold values from -1.75 to 1.75
- second_gain: bfloat16 [768], P('fsdp'), may hold values from 0.5 to 1.5
- second_shift: bfloat16 [768], P('fsdp'), may hold values from -1.75 to 1.75
- triple_weight: bfloat16 [768, 2304], P('fsdp'), may hold values from -0.21875 to 0.21875
- triple_bias: bfloat16 [2304], P('fsdp'), may hold values from -3 to 3
- output_weight: bfloat16 [768, 768], P('fsdp'), may hold values from -1.75 to 1.75
- output_bias: bfloat16 [768], P('fsdp'), may hold values from -1.75 to 1.75
- upward_weight: bfloat16 [768, 3072], P('fsdp'), may hold values from -0.21875 to 0.21875
- upward_bias: bfloat16 [3072], P('fsdp'), may hold values from -3 to 3
- downward_weight: bfloat16 [3072, 768], P('fsdp'), may hold values from -0.109375 to 0.109375
- downward_bias: bfloat16 [768], P('fsdp'), may hold values from -1.75 to 1.75
Outputs:
- block_output: bfloat16 [32768, 768], P(('rep', 'fsdp'))
- input_grad: bfloat16 [32768, 768], P(('rep', 'fsdp'))
- first_gain_grad: float32 [768], P('fsdp')
- first_shift_grad: float32 [768], P('fsdp')
- second_gain_grad: float32 [768], P('fsdp')
- second_shift_grad: float32 [768], P('fsdp')
- triple_weight_grad: float32 [768, 2304], P('fsdp')
- triple_bias_grad: float32 [2304], P('fsdp')
- output_weight_grad: float32 [768, 768], P('fsdp')
- output_bias_grad: float32 [768], P('fsdp')
- upward_weight_grad: float32 [768, 3072], P('fsdp')
- upward_bias_grad: float32 [3072], P('fsdp')
- downward_weight_grad: float32 [3072, 768], P('fsdp')
- downward_bias_grad: float32 [768], P('fsdp')
- example_norms: float32 [32], replicated
Inputs may be any that keep to these rules, and one draw needn't show every extreme that they name: `lengths`: A sequence's real tokens fill the front of its 1024 rows; in every draw one sequence has exactly 1024 real tokens and one exactly 128.
All inputs are finite; a program needn't handle non-finite values.
Results may differ from a plain program's by a relative error of at most 0.012.
Values may be sent and summed in bfloat16 or wider, within the bound.
No kernel may reach another device: no remote copies, remote signals or barrier semaphores. Data moves between devices by JAX's collectives and lax.ppermute only.
A program may use at most 192 MiB of HBM per device.

v0:
```python
from functools import partial
from functools import reduce
import math

import jax
import jax.numpy as jnp
from jax import lax
from jax.sharding import PartitionSpec as P

HEADS = 12
HEAD_DIM = 64
ROT = 16


epsilon = 1e-05
masked_score = -1e30


def layer_norm(values, norm_gain, norm_shift):
    centred = values - jnp.mean(values, axis=-1, keepdims=True)
    variance = jnp.mean(centred * centred, axis=-1, keepdims=True)
    inverse = lax.rsqrt(variance + epsilon)
    normed = centred * inverse
    return (normed * norm_gain + norm_shift, normed, inverse)


def norm_backward(grad_out, norm_gain, normed, inverse):
    scaled = grad_out * norm_gain
    scaled_mean = jnp.mean(scaled, axis=-1, keepdims=True)
    cross_mean = jnp.mean(scaled * normed, axis=-1, keepdims=True)
    grad_in = inverse * (scaled - scaled_mean - normed * cross_mean)
    return (grad_in, jnp.sum(grad_out * normed, axis=0), jnp.sum(grad_out, axis=0))


def rotary_tables(row_count):
    halfway = ROT // 2
    frequency = jnp.exp(jnp.arange(halfway, dtype=jnp.float32) * (-2.0 * math.log(10000.0) / ROT))
    angles = jnp.arange(row_count, dtype=jnp.float32)[:, None] * frequency[None, :]
    cosine_table = jnp.concatenate([jnp.cos(angles), jnp.cos(angles)], axis=1)[:, None, :]
    sine_table = jnp.concatenate([jnp.sin(angles), jnp.sin(angles)], axis=1)[:, None, :]
    return (cosine_table, sine_table)


def rotate(values, cosine_table, sine_table):
    halfway = ROT // 2
    leading = values[..., :ROT]
    turned = jnp.concatenate([-leading[..., halfway:], leading[..., :halfway]], axis=-1)
    return jnp.concatenate(
        [leading * cosine_table + turned * sine_table, values[..., ROT:]], axis=-1
    )


def unrotate(gradient, cosine_table, sine_table):
    halfway = ROT // 2
    leading = gradient[..., :ROT]
    sine_part = leading * sine_table
    turned = jnp.concatenate([sine_part[..., halfway:], -sine_part[..., :halfway]], axis=-1)
    return jnp.concatenate([leading * cosine_table + turned, gradient[..., ROT:]], axis=-1)


def allowed_keys(offset, block_rows, row_count, seq_limit):
    query_pos = offset + jnp.arange(block_rows)[:, None]
    key_pos = jnp.arange(row_count)[None, :]
    return (key_pos <= query_pos) & (key_pos < seq_limit)


def per_device(
    block_input,
    cotangent,
    lengths,
    first_gain,
    first_shift,
    second_gain,
    second_shift,
    triple_weight,
    triple_bias,
    output_weight,
    output_bias,
    upward_weight,
    upward_bias,
    downward_weight,
    downward_bias,
):
    (
        gain_one,
        shift_one,
        gain_two,
        shift_two,
        weight_triple,
        bias_triple,
        weight_output,
        bias_output,
        weight_upward,
        bias_upward,
        weight_downward,
        bias_downward,
    ) = (
        lax.all_gather(first_gain, "fsdp", axis=0, tiled=True),
        lax.all_gather(first_shift, "fsdp", axis=0, tiled=True),
        lax.all_gather(second_gain, "fsdp", axis=0, tiled=True),
        lax.all_gather(second_shift, "fsdp", axis=0, tiled=True),
        lax.all_gather(triple_weight, "fsdp", axis=0, tiled=True),
        lax.all_gather(triple_bias, "fsdp", axis=0, tiled=True),
        lax.all_gather(output_weight, "fsdp", axis=0, tiled=True),
        lax.all_gather(output_bias, "fsdp", axis=0, tiled=True),
        lax.all_gather(upward_weight, "fsdp", axis=0, tiled=True),
        lax.all_gather(upward_bias, "fsdp", axis=0, tiled=True),
        lax.all_gather(downward_weight, "fsdp", axis=0, tiled=True),
        lax.all_gather(downward_bias, "fsdp", axis=0, tiled=True),
    )
    row_count = block_input.shape[0]
    seq_limit = lengths[0]
    valid = (jnp.arange(row_count) < seq_limit).astype(jnp.float32)[:, None]
    source = block_input.astype(jnp.float32)
    first_full, first_norm, first_inverse = layer_norm(
        source, gain_one.astype(jnp.float32), shift_one.astype(jnp.float32)
    )
    first_low = first_full.astype(jnp.bfloat16)
    triple = jnp.dot(
        first_low, weight_triple, preferred_element_type=jnp.float32
    ) + bias_triple.astype(jnp.float32)
    triple_split = triple.reshape(row_count, 3, HEADS, HEAD_DIM)
    cosine_table, sine_table = rotary_tables(row_count)
    query_low = rotate(triple_split[:, 0], cosine_table, sine_table).astype(jnp.bfloat16)
    key_low = rotate(triple_split[:, 1], cosine_table, sine_table).astype(jnp.bfloat16)
    value_low = triple_split[:, 2].astype(jnp.bfloat16)
    block_rows = min(512, row_count)
    block_count = row_count // block_rows
    score_scale = HEAD_DIM ** (-0.5)

    def block_scores(offset):
        query_part = lax.dynamic_slice_in_dim(query_low, offset, block_rows, 0)
        scores = (
            jnp.einsum("qhd,khd->hqk", query_part, key_low, preferred_element_type=jnp.float32)
            * score_scale
        )
        allowed = allowed_keys(offset, block_rows, row_count, seq_limit)
        return (query_part, jnp.where(allowed[None], scores, masked_score))

    def attend_forward(number):
        query_part, scores = block_scores(number * block_rows)
        row_peak = jnp.max(scores, axis=-1, keepdims=True)
        exponent = jnp.exp(scores - row_peak)
        row_total = jnp.sum(exponent, axis=-1, keepdims=True)
        weights_low = (exponent / row_total).astype(jnp.bfloat16)
        context = jnp.einsum(
            "hqk,khd->qhd", weights_low, value_low, preferred_element_type=jnp.float32
        )
        return (context, row_peak[..., 0] + jnp.log(row_total[..., 0]))

    contexts, log_totals = lax.map(attend_forward, jnp.arange(block_count))
    context_low = contexts.reshape(row_count, HEADS * HEAD_DIM).astype(jnp.bfloat16)
    attention_out = jnp.dot(
        context_low, weight_output, preferred_element_type=jnp.float32
    ) + bias_output.astype(jnp.float32)
    second_full, second_norm, second_inverse = layer_norm(
        source, gain_two.astype(jnp.float32), shift_two.astype(jnp.float32)
    )
    second_low = second_full.astype(jnp.bfloat16)
    upward = jnp.dot(
        second_low, weight_upward, preferred_element_type=jnp.float32
    ) + bias_upward.astype(jnp.float32)
    active_low = jax.nn.gelu(upward, approximate=False).astype(jnp.bfloat16)
    mixer_out = jnp.dot(
        active_low, weight_downward, preferred_element_type=jnp.float32
    ) + bias_downward.astype(jnp.float32)
    block_output = ((source + attention_out + mixer_out) * valid).astype(jnp.bfloat16)
    back_gain_one, back_gain_two, back_triple, back_output, back_upward, back_downward = (
        lax.all_gather(first_gain, "fsdp", axis=0, tiled=True),
        lax.all_gather(second_gain, "fsdp", axis=0, tiled=True),
        lax.all_gather(triple_weight, "fsdp", axis=0, tiled=True),
        lax.all_gather(output_weight, "fsdp", axis=0, tiled=True),
        lax.all_gather(upward_weight, "fsdp", axis=0, tiled=True),
        lax.all_gather(downward_weight, "fsdp", axis=0, tiled=True),
    )
    grad_rows = cotangent.astype(jnp.float32) * valid
    grad_low = grad_rows.astype(jnp.bfloat16)
    grad_down_w = jnp.einsum("tf,td->fd", active_low, grad_low, preferred_element_type=jnp.float32)
    grad_down_b = jnp.sum(grad_rows, axis=0)
    grad_active = jnp.einsum(
        "td,fd->tf", grad_low, back_downward, preferred_element_type=jnp.float32
    )
    gelu_back = jax.vjp(partial(jax.nn.gelu, approximate=False), upward)[1]
    grad_upward = gelu_back(grad_active)[0].astype(jnp.bfloat16)
    grad_up_w = jnp.einsum("td,tf->df", second_low, grad_upward, preferred_element_type=jnp.float32)
    grad_up_b = jnp.sum(grad_upward.astype(jnp.float32), axis=0)
    grad_second = jnp.einsum(
        "tf,df->td", grad_upward, back_upward, preferred_element_type=jnp.float32
    )
    from_second, grad_gain_two, grad_shift_two = norm_backward(
        grad_second, back_gain_two.astype(jnp.float32), second_norm, second_inverse
    )
    grad_out_w = jnp.einsum("te,td->ed", context_low, grad_low, preferred_element_type=jnp.float32)
    grad_context = jnp.einsum(
        "td,ed->te", grad_low, back_output, preferred_element_type=jnp.float32
    )
    grad_context = grad_context.astype(jnp.bfloat16).reshape(row_count, HEADS, HEAD_DIM)

    def attend_backward(running, number):
        key_total, value_total = running
        offset = number * block_rows
        query_part, scores = block_scores(offset)
        log_part = lax.dynamic_index_in_dim(log_totals, number, 0, keepdims=False)
        weights_full = jnp.exp(scores - log_part[..., None])
        weights_low = weights_full.astype(jnp.bfloat16)
        grad_part = lax.dynamic_slice_in_dim(grad_context, offset, block_rows, 0)
        grad_weights = jnp.einsum(
            "qhd,khd->hqk", grad_part, value_low, preferred_element_type=jnp.float32
        )
        inner_sum = jnp.sum(weights_full * grad_weights, axis=-1, keepdims=True)
        grad_scores = (weights_full * (grad_weights - inner_sum)).astype(jnp.bfloat16)
        grad_query = (
            jnp.einsum("hqk,khd->qhd", grad_scores, key_low, preferred_element_type=jnp.float32)
            * score_scale
        )
        key_total = (
            key_total
            + jnp.einsum(
                "hqk,qhd->khd", grad_scores, query_part, preferred_element_type=jnp.float32
            )
            * score_scale
        )
        value_total = value_total + jnp.einsum(
            "hqk,qhd->khd", weights_low, grad_part, preferred_element_type=jnp.float32
        )
        return ((key_total, value_total), grad_query)

    zero_grad = jnp.zeros((row_count, HEADS, HEAD_DIM), jnp.float32)
    (grad_key, grad_value), grad_queries = lax.scan(
        attend_backward, (zero_grad, zero_grad), jnp.arange(block_count)
    )
    grad_query = grad_queries.reshape(row_count, HEADS, HEAD_DIM)
    grad_triple = jnp.stack(
        [
            unrotate(grad_query, cosine_table, sine_table),
            unrotate(grad_key, cosine_table, sine_table),
            grad_value,
        ],
        axis=1,
    )
    grad_triple = grad_triple.reshape(row_count, 3 * HEADS * HEAD_DIM).astype(jnp.bfloat16)
    grad_triple_w = jnp.einsum(
        "td,tc->dc", first_low, grad_triple, preferred_element_type=jnp.float32
    )
    grad_triple_b = jnp.sum(grad_triple.astype(jnp.float32), axis=0)
    grad_first = jnp.einsum(
        "tc,dc->td", grad_triple, back_triple, preferred_element_type=jnp.float32
    )
    from_first, grad_gain_one, grad_shift_one = norm_backward(
        grad_first, back_gain_one.astype(jnp.float32), first_norm, first_inverse
    )
    input_grad = (grad_rows + from_first + from_second).astype(jnp.bfloat16)
    grads_local = [
        grad_gain_one,
        grad_shift_one,
        grad_gain_two,
        grad_shift_two,
        grad_triple_w,
        grad_triple_b,
        grad_out_w,
        grad_down_b,
        grad_up_w,
        grad_up_b,
        grad_down_w,
        grad_down_b,
    ]
    square_total = reduce(
        lambda left, right: left + right, [jnp.sum(piece * piece) for piece in grads_local]
    )
    own_norm = jnp.sqrt(square_total).reshape(1)
    example_norms = lax.all_gather(own_norm, ("rep", "fsdp"), axis=0, tiled=True)
    factor = jnp.minimum(1.0, jnp.mean(example_norms) / own_norm[0]) / example_norms.shape[0]
    scaled = [piece * factor for piece in grads_local]
    shard_sums = (
        lax.psum_scatter(scaled[0], "fsdp", scatter_dimension=0, tiled=True),
        lax.psum_scatter(scaled[1], "fsdp", scatter_dimension=0, tiled=True),
        lax.psum_scatter(scaled[2], "fsdp", scatter_dimension=0, tiled=True),
        lax.psum_scatter(scaled[3], "fsdp", scatter_dimension=0, tiled=True),
        lax.psum_scatter(scaled[4], "fsdp", scatter_dimension=0, tiled=True),
        lax.psum_scatter(scaled[5], "fsdp", scatter_dimension=0, tiled=True),
        lax.psum_scatter(scaled[6], "fsdp", scatter_dimension=0, tiled=True),
        lax.psum_scatter(scaled[7], "fsdp", scatter_dimension=0, tiled=True),
        lax.psum_scatter(scaled[8], "fsdp", scatter_dimension=0, tiled=True),
        lax.psum_scatter(scaled[9], "fsdp", scatter_dimension=0, tiled=True),
        lax.psum_scatter(scaled[10], "fsdp", scatter_dimension=0, tiled=True),
        lax.psum_scatter(scaled[11], "fsdp", scatter_dimension=0, tiled=True),
    )
    final = (
        lax.psum(shard_sums[0].astype(jnp.bfloat16), "rep").astype(jnp.float32),
        lax.psum(shard_sums[1].astype(jnp.bfloat16), "rep").astype(jnp.float32),
        lax.psum(shard_sums[2].astype(jnp.bfloat16), "rep").astype(jnp.float32),
        lax.psum(shard_sums[3].astype(jnp.bfloat16), "rep").astype(jnp.float32),
        lax.psum(shard_sums[4].astype(jnp.bfloat16), "rep").astype(jnp.float32),
        lax.psum(shard_sums[5].astype(jnp.bfloat16), "rep").astype(jnp.float32),
        lax.psum(shard_sums[6].astype(jnp.bfloat16), "rep").astype(jnp.float32),
        lax.psum(shard_sums[7].astype(jnp.bfloat16), "rep").astype(jnp.float32),
        lax.psum(shard_sums[8].astype(jnp.bfloat16), "rep").astype(jnp.float32),
        lax.psum(shard_sums[9].astype(jnp.bfloat16), "rep").astype(jnp.float32),
        lax.psum(shard_sums[10].astype(jnp.bfloat16), "rep").astype(jnp.float32),
        lax.psum(shard_sums[11].astype(jnp.bfloat16), "rep").astype(jnp.float32),
    )
    return (
        block_output,
        input_grad,
        final[0],
        final[1],
        final[2],
        final[3],
        final[4],
        final[5],
        final[6],
        final[7],
        final[8],
        final[9],
        final[10],
        final[11],
        example_norms,
    )


def solution(mesh):
    return jax.shard_map(
        per_device,
        mesh=mesh,
        in_specs=(
            P(("rep", "fsdp"), None),
            P(("rep", "fsdp"), None),
            P(("rep", "fsdp")),
            P("fsdp"),
            P("fsdp"),
            P("fsdp"),
            P("fsdp"),
            P("fsdp", None),
            P("fsdp"),
            P("fsdp", None),
            P("fsdp"),
            P("fsdp", None),
            P("fsdp"),
            P("fsdp", None),
            P("fsdp"),
        ),
        out_specs=(
            P(("rep", "fsdp"), None),
            P(("rep", "fsdp"), None),
            P("fsdp"),
            P("fsdp"),
            P("fsdp"),
            P("fsdp"),
            P("fsdp", None),
            P("fsdp"),
            P("fsdp", None),
            P("fsdp"),
            P("fsdp", None),
            P("fsdp"),
            P("fsdp", None),
            P("fsdp"),
            P(),
        ),
        check_vma=False,
    )
```

profile of v0, /device:TPU:0, one launch (start us, length us, event | category | flops | bytes accessed | tf_op | source)
XLA Modules:
  0.0 986.6 jit_solution(13106800385008307129)
XLA Ops:
  18.7 31.1 %all-reduce.16 = (bf16[768]{0:T(1024)(128)(2,1)S(1)}, bf16[768]{0:T(1024)(128)(2,1)S(1)}, bf16[2304]{0:T(1024)(128)(2,1)S(1)}, bf16[768]{0:T(1024)(128)(2,1)S(1)...) all-reduce(bf16[768]{0:T(1024)(128)(2,1)S(1)} %dynamic-update-slice, ...), channel_id=1, replica_groups=mesh['rep'=4,'fsdp'=8] {'fsdp'}, use_global_device_ids=true, to_apply=%add.5 | all-reduce | flops 6912 | bytes 27648
  54.2 13.2 %all-gather = bf16[8,1,384]{2,1,0:T(2,128)(2,1)S(1)} all-gather(bf16[1,1,384]{2,1,0:T(2,128)(2,1)S(1)} %reshape.236), channel_id=1, replica_groups=mesh['rep'=4,'fsdp'=8] {'fsdp'}, dimensions={0}, use_global_device_ids=true | all-gather | bytes 6912 | tf_op jit(solution)/shard_map/all_gather | solution.py:107
  87.1 9.8 copy.39
  104.9 74.6 %while.27 = (s32[]{:T(128)}, bf16[2,512,12,64]{1,3,2,0:T(8,128)(2,1)}, f32[2,12,512]{2,1,0:T(8,128)S(1)}, s32[2]{0:T(128)S(1)}, s32[]{:T(128)}, /*index=5*/bf16[...) while((s32[]{:T(128)}, ...), condition=%wide.region_5.6_spmd, body=%wide.region_2.5_spmd.sunk | while | flops 1687154176 | bytes 190282480 | solution.py:151
  107.3 10.7 %fusion.134 = (f32[12,512]{1,0:T(8,128)S(1)}, f32[12,512,1024]{2,1,0:T(8,128)}) fusion(pred[512,1024]{1,0:T(8,128)(4,1)S(1)} %fusion.133, bf16[1024,12,64]{0,2,1:T(8,128)(2,1)S(1)} %get-tuple-element.433, bf16[1024,12,64]{0,2,1:T(8,128)(2,1)S(1)} %get-tuple-element.432, s32[]{:T(128)S(6)} %select_n.55), kind=kOutput, calls=%fused_computation.3.clone.1 | convolution fusion | flops 824174592 | bytes 28073988 | tf_op jit(solution)/shard_map/while/body/eval_jaxpr/qhd,khd->hqk/dot_general | solution.py:134
  118.0 12.4 %fusion.135 = f32[12,512]{1,0:T(8,128)S(1)} fusion(f32[12,512,1024]{2,1,0:T(8,128)} %get-tuple-element.388, f32[12,512]{1,0:T(8,128)S(1)} %get-tuple-element.389, pred[512,1024]{1,0:T(8,128)(4,1)S(1)} %fusion.133), kind=kLoop, calls=%fused_computation.4.clone.1 | loop fusion | flops 25159680 | bytes 25739264 | tf_op jit(solution)/shard_map/while/body/eval_jaxpr/reduce_sum | solution.py:144
  144.4 10.8 %fusion.134 = (f32[12,512]{1,0:T(8,128)S(1)}, f32[12,512,1024]{2,1,0:T(8,128)}) fusion(pred[512,1024]{1,0:T(8,128)(4,1)S(1)} %fusion.133, bf16[1024,12,64]{0,2,1:T(8,128)(2,1)S(1)} %get-tuple-element.433, bf16[1024,12,64]{0,2,1:T(8,128)(2,1)S(1)} %get-tuple-element.432, s32[]{:T(128)S(6)} %select_n.55), kind=kOutput, calls=%fused_computation.3.clone.1 | convolution fusion | flops 824174592 | bytes 28073988 | tf_op jit(solution)/shard_map/while/body/eval_jaxpr/qhd,khd->hqk/dot_general | solution.py:134
  155.1 12.4 %fusion.135 = f32[12,512]{1,0:T(8,128)S(1)} fusion(f32[12,512,1024]{2,1,0:T(8,128)} %get-tuple-element.388, f32[12,512]{1,0:T(8,128)S(1)} %get-tuple-element.389, pred[512,1024]{1,0:T(8,128)(4,1)S(1)} %fusion.133), kind=kLoop, calls=%fused_computation.4.clone.1 | loop fusion | flops 25159680 | bytes 25739264 | tf_op jit(solution)/shard_map/while/body/eval_jaxpr/reduce_sum | solution.py:144
  179.5 238.2 %while.28 = (s32[]{:T(128)}, f32[1024,12,64]{0,2,1:T(8,128)}, f32[1024,12,64]{0,2,1:T(8,128)}, f32[2,512,12,64]{1,0,3,2:T(2,128)}, s32[2]{0:T(128)S(1)}, /*index...) while((s32[]{:T(128)}, f32[1024,12,64]{0,2,1:T(8,128)}, ...), condition=%wide.region_8.9_spmd.clone, body=%wide.region_6.8_spmd.clone.sunk | while | flops 4126273024 | bytes 242407856 | solution.py:229
  181.2 10.1 %fusion.145 = f32[12,512,1024]{2,1,0:T(8,128)} fusion(bf16[1024,12,64]{0,2,1:T(8,128)(2,1)S(1)} %get-tuple-element.478, bf16[1024,12,64]{0,2,1:T(8,128)(2,1)S(1)} %get-tuple-element.476, s32[]{:T(128)S(6)} %select_n.59), kind=kOutput, calls=%fused_computation.32.clone.1 | convolution fusion | flops 805306368 | bytes 27525124 | tf_op jit(solution)/shard_map/while/body/eval_jaxpr/qhd,khd->hqk/dot_general | solution.py:134
  194.4 18.3 %multiply_reduce_fusion.15 = (f32[12,512]{1,0:T(8,128)S(1)}, f32[12,512,1024]{2,1,0:T(8,128)}) fusion(f32[12,512,1024]{2,1,0:T(8,128)} %fusion.145, f32[12,512]{1,0:T(8,128)S(1)} %dynamic-slice_bitcast_fusion.2, pred[512,1024]{1,0:T(8,128)(4,1)S(1)} %fusion.146, bf16[1024,12,64]{0,2,1:T(8,128)(2,1)} %get-tuple-element.481, ...), kind=kOutput, calls=%fused_computation.18.clone.1 | convolution fusion | flops 836757504 | bytes 53264388 | tf_op jit(solution)/shard_map/while/body/eval_jaxpr/qhd,khd->hqk/dot_general | solution.py:207
  212.6 21.2 %multiply_convert_fusion.3 = bf16[12,512,1024]{2,1,0:T(8,128)(2,1)} fusion(f32[12,512,1024]{2,1,0:T(8,128)} %get-tuple-element.401, f32[12,512,1024]{2,1,0:T(8,128)} %fusion.145, f32[12,512]{1,0:T(8,128)S(1)} %get-tuple-element.402, f32[12,512]{1,0:T(8,128)S(1)} %dynamic-slice_bitcast_fusion.2, pred[512,1024]{1,0:T(8,128)(4,1)S(1)} %fusion.146), kind=kLoop, calls=%fused_computation.17.clone.1 | loop fusion | flops 37748736 | bytes 63488000 | tf_op jit(solution)/shard_map/while/body/eval_jaxpr/convert_element_type | solution.py:211
  233.9 9.7 multiply_bitcast_fusion.2
  246.6 28.7 %dynamic_update_slice.19 = f32[2,512,12,64]{1,0,3,2:T(2,128)} dynamic-update-slice(f32[2,512,12,64]{1,0,3,2:T(2,128)} %get-tuple-element.458, f32[1,512,12,64]{1,0,3,2:T(1,128)S(1)} %copy.71, s32[]{:T(128)} %get-tuple-element.455, s32[]{:T(128)} %constant.72.clone.1..sunk.1, s32[]{:T(128)} %constant.72.clone.1..sunk.1, s32[]{:T(128)} %constant.72.clone.1..sunk.1) | dynamic-update-slice | bytes 3145732 | tf_op jit(solution)/shard_map/while/body/jit(dynamic_update_index_in_dim)/dynamic_update_slice | solution.py:151
  284.2 13.6 %bitcast_add_fusion.5 = f32[1024,12,64]{0,2,1:T(8,128)} fusion(f32[1024,12,64]{0,2,1:T(8,128)} %get-tuple-element.457, f32[12,512,1024]{2,1,0:T(8,128)} %fusion.145, f32[12,512]{1,0:T(8,128)S(1)} %dynamic-slice_bitcast_fusion.2, pred[512,1024]{1,0:T(8,128)(4,1)S(1)} %copy-done.3, pred[]{:T(512)S(6)} %compare.3, ...), kind=kOutput, calls=%fused_computation.23.clone.1 | convolution fusion | flops 832045056 | bytes 32800772 | tf_op jit(solution)/shard_map/while/body/eval_jaxpr/hqk,qhd->khd/dot_general | solution.py:223
  299.2 10.1 %fusion.145 = f32[12,512,1024]{2,1,0:T(8,128)} fusion(bf16[1024,12,64]{0,2,1:T(8,128)(2,1)S(1)} %get-tuple-element.478, bf16[1024,12,64]{0,2,1:T(8,128)(2,1)S(1)} %get-tuple-element.476, s32[]{:T(128)S(6)} %select_n.59), kind=kOutput, calls=%fused_computation.32.clone.1 | convolution fusion | flops 805306368 | bytes 27525124 | tf_op jit(solution)/shard_map/while/body/eval_jaxpr/qhd,khd->hqk/dot_general | solution.py:134
  312.3 18.3 %multiply_reduce_fusion.15 = (f32[12,512]{1,0:T(8,128)S(1)}, f32[12,512,1024]{2,1,0:T(8,128)}) fusion(f32[12,512,1024]{2,1,0:T(8,128)} %fusion.145, f32[12,512]{1,0:T(8,128)S(1)} %dynamic-slice_bitcast_fusion.2, pred[512,1024]{1,0:T(8,128)(4,1)S(1)} %fusion.146, bf16[1024,12,64]{0,2,1:T(8,128)(2,1)} %get-tuple-element.481, ...), kind=kOutput, calls=%fused_computation.18.clone.1 | convolution fusion | flops 836757504 | bytes 53264388 | tf_op jit(solution)/shard_map/while/body/eval_jaxpr/qhd,khd->hqk/dot_general | solution.py:207
  330.6 21.2 %multiply_convert_fusion.3 = bf16[12,512,1024]{2,1,0:T(8,128)(2,1)} fusion(f32[12,512,1024]{2,1,0:T(8,128)} %get-tuple-element.401, f32[12,512,1024]{2,1,0:T(8,128)} %fusion.145, f32[12,512]{1,0:T(8,128)S(1)} %get-tuple-element.402, f32[12,512]{1,0:T(8,128)S(1)} %dynamic-slice_bitcast_fusion.2, pred[512,1024]{1,0:T(8,128)(4,1)S(1)} %fusion.146), kind=kLoop, calls=%fused_computation.17.clone.1 | loop fusion | flops 37748736 | bytes 63488000 | tf_op jit(solution)/shard_map/while/body/eval_jaxpr/convert_element_type | solution.py:211
  351.8 9.7 multiply_bitcast_fusion.2
  364.6 28.7 %dynamic_update_slice.19 = f32[2,512,12,64]{1,0,3,2:T(2,128)} dynamic-update-slice(f32[2,512,12,64]{1,0,3,2:T(2,128)} %get-tuple-element.458, f32[1,512,12,64]{1,0,3,2:T(1,128)S(1)} %copy.71, s32[]{:T(128)} %get-tuple-element.455, s32[]{:T(128)} %constant.72.clone.1..sunk.1, s32[]{:T(128)} %constant.72.clone.1..sunk.1, s32[]{:T(128)} %constant.72.clone.1..sunk.1) | dynamic-update-slice | bytes 3145732 | tf_op jit(solution)/shard_map/while/body/jit(dynamic_update_index_in_dim)/dynamic_update_slice | solution.py:151
  393.3 9.8 bitcast_add_fusion.4
  403.1 14.5 %bitcast_add_fusion.5 = f32[1024,12,64]{0,2,1:T(8,128)} fusion(f32[1024,12,64]{0,2,1:T(8,128)} %get-tuple-element.457, f32[12,512,1024]{2,1,0:T(8,128)} %fusion.145, f32[12,512]{1,0:T(8,128)S(1)} %dynamic-slice_bitcast_fusion.2, pred[512,1024]{1,0:T(8,128)(4,1)S(1)} %copy-done.3, pred[]{:T(512)S(6)} %compare.3, ...), kind=kOutput, calls=%fused_computation.23.clone.1 | convolution fusion | flops 832045056 | bytes 32800772 | tf_op jit(solution)/shard_map/while/body/eval_jaxpr/hqk,qhd->khd/dot_general | solution.py:223
  445.7 36.2 %multiply_convert_fusion.1 = (bf16[1024,3072]{1,0:T(8,128)(2,1)}, f32[1024,3072]{1,0:T(8,128)}, f32[1024,3072]{1,0:T(8,128)}) fusion(f32[3072]{0:T(1024)S(1)} %bitcast.109, bf16[768,3072]{1,0:T(8,128)(2,1)} %all-gather.10.cloned.1.call-done, bf16[1024,768]{1,0:T(8,128)(2,1)S(1)} %copy-done.8, f32[768]{0:T(1024)S(1)} %copy-done.34, f32[768]{0:T(1024)S(1)} %copy-done.32, ...), kind=kOutput, calls=%fused_computation.47 | convolution fusion | flops 5044174848 | bytes 37775360 | tf_op jit(solution)/shard_map/dot_general | solution.py:160
  481.9 16.8 %convert_reduce_fusion = (f32[3072]{0:T(1024)S(1)}, bf16[1024,3072]{1,0:T(8,128)(2,1)}) fusion(f32[1024,3072]{1,0:T(8,128)} %get-tuple-element.236, bf16[3072,768]{1,0:T(8,128)(2,1)} %all-gather.12.cloned.1.call-done, bf16[1024,768]{1,0:T(8,128)(2,1)S(1)} %copy-done.12, f32[1024]{0:T(1024)S(1)} %copy-done.27, f32[1024,3072]{1,0:T(8,128)} %get-tuple-element.263, ...), kind=kOutput, calls=%fused_computation.45 | convolution fusion | flops 4887671808 | bytes 37777408 | tf_op jit(solution)/shard_map/td,fd->tf/dot_general | solution.py:180
  498.7 12.4 %multiply_reduce_fusion.2 = (f32[]{:T(128)}, f32[768,3072]{1,0:T(8,128)}) fusion(bf16[1024,3072]{1,0:T(8,128)(2,1)} %get-tuple-element.272, bf16[1024,768]{1,0:T(8,128)(2,1)S(1)} %copy-done.8, f32[768]{0:T(1024)S(1)} %copy-done.34, f32[768]{0:T(1024)S(1)} %copy-done.32, f32[1024]{0:T(1024)S(1)} %copy-done.31, f32[1024]{0:T(1024)S(1)} %copy-done.25), kind=kOutput, calls=%fused_computation.63 | convolution fusion | flops 4841275392 | bytes 17315844 | tf_op jit(solution)/shard_map/td,tf->df/dot_general | solution.py:185
  546.3 39.0 %all-reduce.7 = f32[32]{0:T(128)S(1)} all-reduce(f32[32]{0:T(128)S(1)} %dynamic-update-slice.7), channel_id=1, replica_groups=mesh['rep'=4,'fsdp'=8] {'rep','fsdp'}, use_global_device_ids=true, to_apply=%add.7 | all-reduce | flops 32 | bytes 256
  615.8 27.8 %all-reduce.15 = (bf16[768]{0:T(1024)(128)(2,1)S(1)}, bf16[768]{0:T(1024)(128)(2,1)S(1)}, bf16[768]{0:T(1024)(128)(2,1)S(1)}, bf16[768]{0:T(1024)(128)(2,1)S(1)}...) all-reduce(f32[768]{0:T(1024)S(1)} %broadcast_multiply_fusion.10, ...), channel_id=2, replica_groups=mesh['rep'=4,'fsdp'=8] {'fsdp'}, use_global_device_ids=true, to_apply=%region_32.33.clone | all-reduce | flops 9216 | bytes 55296
  644.1 9.8 all-reduce.17
  658.8 46.5 %reduce-scatter.5.cloned.1.call-done = f32[96,2304]{1,0:T(8,128)} async-done(((f32[768,2304]{1,0:T(8,128)}), f32[96,2304]{1,0:T(8,128)}) %reduce-scatter.5.cloned.1.call-update) | async-done | bytes 884752 | tf_op jit(solution)/shard_map/reduce_scatter | solution.py:279
  707.3 98.0 %reduce-scatter.11.cloned.1.call-done = f32[384,768]{1,0:T(8,128)} async-done(((f32[3072,768]{1,0:T(8,128)}), f32[384,768]{1,0:T(8,128)}) %reduce-scatter.11.cloned.1.call-update) | async-done | bytes 1179664 | tf_op jit(solution)/shard_map/reduce_scatter | solution.py:285
  807.5 98.1 %reduce-scatter.9.cloned.1.call-done = f32[96,3072]{1,0:T(8,128)} async-done(((f32[768,3072]{1,0:T(8,128)}), f32[96,3072]{1,0:T(8,128)}) %reduce-scatter.9.cloned.1.call-update) | async-done | bytes 1179664 | tf_op jit(solution)/shard_map/reduce_scatter | solution.py:283
  919.4 53.9 %all-reduce.21.cloned.1.call-done = (bf16[96,2304]{1,0:T(8,128)(2,1)}, bf16[96,768]{1,0:T(8,128)(2,1)}, bf16[96,3072]{1,0:T(8,128)(2,1)}, bf16[384,768]{1,0:T(8,128)(2,1)}) async-done(((bf16[96,2304]{1,0:T(8,128)(2,1)}, bf16[96,768]{1,0:T(8,128)(2,1)}, bf16[96,3072]{1,0:T(8,128)(2,1)}, bf16[384,768]{1,0:T(8,128)(2,1)}), (bf16[96,2304]{1,0:T(8,128)(2,1)}, bf16[96,768]{1,0:T(8,128)(2,1)}, ...) | async-done | bytes 1769488 | tf_op jit(solution)/shard_map/psum | solution.py:293
  (282 shorter events, 199.4 us)
Async XLA Ops:
  7.2 44.3 %copy-start.7 = (bf16[1024,768]{1,0:T(8,128)(2,1)S(1)}, bf16[1024,768]{1,0:T(8,128)(2,1)}, u32[]{:S(2)}) copy-start(bf16[1024,768]{1,0:T(8,128)(2,1)} %param.19) | copy-start | bytes 4718596
  7.2 47.0 %copy-start.39 = (bf16[384]{0:T(512)(128)(2,1)S(1)}, bf16[384]{0:T(512)(128)(2,1)}, u32[]{:S(2)}) copy-start(bf16[384]{0:T(512)(128)(2,1)} %param.31) | copy-start | bytes 2308
  7.2 60.9 %copy-start.11 = (bf16[1024,768]{1,0:T(8,128)(2,1)S(1)}, bf16[1024,768]{1,0:T(8,128)(2,1)}, u32[]{:S(2)}) copy-start(bf16[1024,768]{1,0:T(8,128)(2,1)} %param.20) | copy-start | bytes 4718596
  7.2 60.9 %all-gather.8.cloned.1.call-start = ((), (), s32[]{:S(2)}) async-start(), calls=%async_computation.5 | async-start | bytes 1327104 | tf_op jit(solution)/shard_map/all_gather | solution.py:104
  7.9 70.4 %all-gather.6.cloned.1.call-start = ((), (), s32[]{:S(2)}) async-start(), calls=%async_computation.4 | async-start | bytes 3981312 | tf_op jit(solution)/shard_map/all_gather | solution.py:102
  8.7 437.0 %all-gather.10.cloned.1.call-start = ((), (), s32[]{:S(2)}) async-start(), calls=%async_computation.6 | async-start | bytes 5308416 | tf_op jit(solution)/shard_map/all_gather | solution.py:106
  9.4 472.5 %all-gather.12.cloned.1.call-start = ((), (), s32[]{:S(2)}) async-start(), calls=%async_computation.7 | async-start | bytes 5308416 | tf_op jit(solution)/shard_map/all_gather | solution.py:108
  10.0 647.1 %reduce-scatter.7.cloned.1.call-start = ((), (), s32[]{:S(2)}) async-start(), calls=%async_computation.9 | async-start | bytes 2654208 | tf_op jit(solution)/shard_map/reduce_scatter | solution.py:281
  49.8 28.6 %copy-start.28 = (f32[768]{0:T(1024)}, f32[768]{0:T(1024)S(1)}, u32[]{:S(2)}) copy-start(f32[768]{0:T(1024)S(1)} %convert_element_type.167) | copy-start | bytes 9220
  49.8 28.6 %copy-start.35 = (f32[768]{0:T(1024)}, f32[768]{0:T(1024)S(1)}, u32[]{:S(2)}) copy-start(f32[768]{0:T(1024)S(1)} %convert_element_type.168) | copy-start | bytes 9220
  51.5 26.9 %copy-start.24 = (f32[1024]{0:T(1024)}, f32[1024]{0:T(1024)S(1)}, u32[]{:S(2)}) copy-start(f32[1024]{0:T(1024)S(1)} %broadcast_multiply_fusion.15) | copy-start | bytes 12292
  52.1 26.3 %copy-start.30 = (f32[1024]{0:T(1024)}, f32[1024]{0:T(1024)S(1)}, u32[]{:S(2)}) copy-start(f32[1024]{0:T(1024)S(1)} %add_rsqrt_fusion) | copy-start | bytes 12292
  53.0 19.1 %copy-start.26 = (f32[1024]{0:T(1024)}, f32[1024]{0:T(1024)S(1)}, u32[]{:S(2)}) copy-start(f32[1024]{0:T(1024)S(1)} %fusion.72) | copy-start | bytes 12292
  68.0 36.2 %copy-start.16 = (f32[1024,16]{0,1:T(8,128)}, f32[1024,16]{0,1:T(8,128)S(1)}, u32[]{:S(2)}) copy-start(f32[1024,16]{0,1:T(8,128)S(1)} %get-tuple-element.277) | copy-start | bytes 196612
  68.1 36.2 %copy-start.18 = (f32[1024,16]{0,1:T(8,128)}, f32[1024,16]{0,1:T(8,128)S(1)}, u32[]{:S(2)}) copy-start(f32[1024,16]{0,1:T(8,128)S(1)} %get-tuple-element.278) | copy-start | bytes 196612
  107.2 23.1 %copy-start.6 = (bf16[1024,12,64]{0,2,1:T(8,128)(2,1)S(1)}, bf16[1024,12,64]{0,2,1:T(8,128)(2,1)}, u32[]{:S(2)}) copy-start(bf16[1024,12,64]{0,2,1:T(8,128)(2,1)} %get-tuple-element.434) | copy-start | bytes 4718596 | tf_op jit(solution)/shard_map/while
  118.0 15.6 %copy-start = (f32[12,512,1024]{2,1,0:T(8,128)S(1)}, f32[12,512,1024]{2,1,0:T(8,128)}, u32[]{:S(2)}) copy-start(f32[12,512,1024]{2,1,0:T(8,128)} %get-tuple-element.388) | copy-start | bytes 75497472 | tf_op jit(solution)/shard_map/while
  144.3 23.2 %copy-start.6 = (bf16[1024,12,64]{0,2,1:T(8,128)(2,1)S(1)}, bf16[1024,12,64]{0,2,1:T(8,128)(2,1)}, u32[]{:S(2)}) copy-start(bf16[1024,12,64]{0,2,1:T(8,128)(2,1)} %get-tuple-element.434) | copy-start | bytes 4718596 | tf_op jit(solution)/shard_map/while
  155.1 15.9 %copy-start = (f32[12,512,1024]{2,1,0:T(8,128)S(1)}, f32[12,512,1024]{2,1,0:T(8,128)}, u32[]{:S(2)}) copy-start(f32[12,512,1024]{2,1,0:T(8,128)} %get-tuple-element.388) | copy-start | bytes 75497472 | tf_op jit(solution)/shard_map/while
  194.4 18.3 %copy-start.2 = (pred[512,1024]{1,0:T(8,128)(4,1)}, pred[512,1024]{1,0:T(8,128)(4,1)S(1)}, u32[]{:S(2)}) copy-start(pred[512,1024]{1,0:T(8,128)(4,1)S(1)} %fusion.146) | copy-start | bytes 1572868 | tf_op jit(solution)/shard_map/while
  284.2 13.6 %copy-start.5 = (bf16[1024,12,64]{0,2,1:T(8,128)(2,1)S(1)}, bf16[1024,12,64]{0,2,1:T(8,128)(2,1)}, u32[]{:S(2)}) copy-start(bf16[1024,12,64]{0,2,1:T(8,128)(2,1)} %copy-done.4) | copy-start | bytes 4718596 | tf_op jit(solution)/shard_map/while
  312.3 18.3 %copy-start.2 = (pred[512,1024]{1,0:T(8,128)(4,1)}, pred[512,1024]{1,0:T(8,128)(4,1)S(1)}, u32[]{:S(2)}) copy-start(pred[512,1024]{1,0:T(8,128)(4,1)S(1)} %fusion.146) | copy-start | bytes 1572868 | tf_op jit(solution)/shard_map/while
  403.1 14.5 %copy-start.5 = (bf16[1024,12,64]{0,2,1:T(8,128)(2,1)S(1)}, bf16[1024,12,64]{0,2,1:T(8,128)(2,1)}, u32[]{:S(2)}) copy-start(bf16[1024,12,64]{0,2,1:T(8,128)(2,1)} %copy-done.4) | copy-start | bytes 4718596 | tf_op jit(solution)/shard_map/while
  431.6 13.4 %copy-start.21 = (f32[3,12,64]{2,1,0:T(8,128)}, f32[3,12,64]{2,1,0:T(8,128)S(1)}, u32[]{:S(2)}) copy-start(f32[3,12,64]{2,1,0:T(8,128)S(1)} %get-tuple-element.233) | copy-start | bytes 27652
  498.6 17.5 %slice-start = ((s8[4718592]{0:T(1024)(128)(4,1)}), s8[4194304]{0:T(1024)(128)(4,1)S(1)}, s32[]{:S(2)}) async-start(s8[4718592]{0:T(1024)(128)(4,1)} %bitcast.104), calls=%async_computation.13 | async-start | bytes 8388608
  511.0 18.2 %slice-start.2 = ((s8[6291456]{0:T(1024)(128)(4,1)}), s8[2097152]{0:T(1024)(128)(4,1)S(1)}, s32[]{:S(2)}) async-start(s8[6291456]{0:T(1024)(128)(4,1)} %bitcast.111), calls=%async_computation.15 | async-start | bytes 4194304
  516.2 13.1 %slice-start.3 = ((s8[6291456]{0:T(1024)(128)(4,1)}), s8[4194304]{0:T(1024)(128)(4,1)S(1)}, s32[]{:S(2)}) async-start(s8[6291456]{0:T(1024)(128)(4,1)} %bitcast.111), calls=%async_computation.16 | async-start | bytes 8388608
  589.9 115.4 %reduce-scatter.5.cloned.1.call-start = ((), (), s32[]{:S(2)}) async-start(), calls=%async_computation.8 | async-start | bytes 7962624 | tf_op jit(solution)/shard_map/reduce_scatter | solution.py:279
  596.4 208.9 %reduce-scatter.11.cloned.1.call-start = ((), (), s32[]{:S(2)}) async-start(), calls=%async_computation.11 | async-start | bytes 10616832 | tf_op jit(solution)/shard_map/reduce_scatter | solution.py:285
  604.5 301.0 %reduce-scatter.9.cloned.1.call-start = ((), (), s32[]{:S(2)}) async-start(), calls=%async_computation.10 | async-start | bytes 10616832 | tf_op jit(solution)/shard_map/reduce_scatter | solution.py:283
  613.6 359.7 %all-reduce.21.cloned.1.call-start = ((), (), s32[]{:S(2)}) async-start(), calls=%async_computation.12 | async-start | bytes 3538944 | tf_op jit(solution)/shard_map/psum | solution.py:293
  655.1 324.3 %copy-start.44 = (f32[96]{0:T(128)}, f32[96]{0:T(128)S(1)}, u32[]{:S(2)}) copy-start(f32[96]{0:T(128)S(1)} %convert_element_type.207) | copy-start | bytes 1156
  (34 other events, 197.3 us)
Sparse Core Ops, SparseCore 0:
  9.7 25.6 all-gather.7
  37.0 41.3 all-gather.5
  80.0 50.5 all-gather.9
  132.2 50.5 all-gather.11
  590.0 36.4 reduce-scatter.6
  628.7 76.5 reduce-scatter.4
  707.6 97.6 reduce-scatter.10
  807.6 97.8 reduce-scatter.8
  910.1 63.1 all-reduce.20
where the time goes:
time: 1000 us; the launch traced here: 987 us
  waiting for transfers between devices  306 us (31%)
  matrix products  283 us (28%)
  other arithmetic  134 us (13%)
  blocking collectives  121 us (12%)
  local copies, waits for them, and re-layouts  109 us (11%)
  between operations  27.2 us (3%)
    reduce_scatter x1, waiting for transfers between devices, per_device(): lax.psum_scatter(scaled[8], 'fsdp', scatter_dimension=0, tiled=True)  98.1 us
    reduce_scatter x1, waiting for transfers between devices, per_device(): lax.psum_scatter(scaled[10], 'fsdp', scatter_dimension=0, tiled=True)  98 us
    unnamed x3, blocking collectives  97.9 us
    dynamic_update_slice x4, local copies, waits for them, and re-layouts, per_device(): contexts, log_totals = lax.map(attend_forward, jnp.arange(block_count))  63.4 us
    psum x1, waiting for transfers between devices, per_device(): lax.psum(shard_sums[4].astype(jnp.bfloat16), 'rep').astype(jnp.float32)  53.9 us
    reduce_scatter x1, waiting for transfers between devices, per_device(): lax.psum_scatter(scaled[4], 'fsdp', scatter_dimension=0, tiled=True)  46.5 us
    convert_element_type x2, other arithmetic, attend_backward(): (weights_full * (grad_weights - inner_sum)).astype(jnp.bfloat16)  42.5 us
    dot_general x4, matrix products, block_scores(): jnp.einsum('qhd,khd->hqk', query_part, key_low, preferred_element_type=jn...  41.7 us
  transfers between devices with their start and end apart: 9, of which 5 were waited for; matrix products, arithmetic and copies ran while one was open for 45% of the time, Pallas kernels for 0%

commit v1 on v0

v1 whole, which is shorter than its diff:
```python
import math
import numpy as np
import jax
import jax.numpy as jnp
from jax import lax
from jax.experimental import pallas as pl
from jax.experimental.pallas import tpu as pltpu
from jax.sharding import PartitionSpec as P

HEADS = 12
HEAD_DIM = 64
ROT = 16
EPS = 1e-05
MASKED = -1e30
BF = jnp.bfloat16
F32 = jnp.float32
GROUPS = 3
VMEM_LIMIT = 60 * 1024 * 1024


def mm(a, b):
    return jnp.dot(a, b, preferred_element_type=F32)


def mm_rt(a, b):
    return lax.dot_general(a, b, (((1,), (1,)), ((), ())), preferred_element_type=F32)


def mm_lt(a, b):
    return lax.dot_general(a, b, (((0,), (0,)), ((), ())), preferred_element_type=F32)


def rotary_tables(rows, width):
    half = ROT // 2
    freq = np.exp(np.arange(half, dtype=np.float32) * np.float32(-2.0 * math.log(10000.0) / ROT))
    ang = np.arange(rows, dtype=np.float32)[:, None] * freq.astype(np.float32)[None, :]
    cos, sin = np.cos(ang), np.sin(ang)
    keep = np.ones((rows, HEAD_DIM), np.float32)
    up = np.zeros((rows, HEAD_DIM), np.float32)
    down = np.zeros((rows, HEAD_DIM), np.float32)
    keep[:, :half] = cos
    keep[:, half:ROT] = cos
    up[:, :half] = -sin
    down[:, half:ROT] = sin
    rep = width // HEAD_DIM
    return tuple(np.tile(t, (1, rep)).astype(np.float32) for t in (keep, up, down))


def norm_parts(values):
    centred = values - jnp.mean(values, axis=-1, keepdims=True)
    inverse = lax.rsqrt(jnp.mean(centred * centred, axis=-1, keepdims=True) + EPS)
    return centred * inverse, inverse


def norm_back(e, gain, normed, inverse):
    t = e * gain
    t_mean = jnp.mean(t, axis=-1, keepdims=True)
    cross = jnp.mean(t * normed, axis=-1, keepdims=True)
    return inverse * (t - t_mean - normed * cross)


def attn_kernel(len_ref, x_ref, g_ref, gain_ref, shift_ref, w3_ref, b3_ref, wo_ref, keep_ref, up_ref, down_ref,
                dw3_ref, dwo_ref, db3_ref, dgain_ref, dshift_ref, sq_ref, ao_ref, ff_ref,
                n1, n1t, gl, gf, q_s, k_s, v_s, dc_s, d3, ctx, dq, dk, dv):
    step = pl.program_id(0)
    last = pl.num_programs(0) - 1
    rows, d = x_ref.shape
    gw = wo_ref.shape[0]
    qb = 256
    nb = rows // qb
    seq = len_ref[0]

    @pl.when(step == 0)
    def _():
        def prep(i, c):
            r = pl.ds(pl.multiple_of(i * qb, qb), qb)
            normed, _ = norm_parts(x_ref[r, :].astype(F32))
            low = normed * gain_ref[...] + shift_ref[...]
            n1[r, :] = low.astype(BF)
            valid = (lax.broadcasted_iota(jnp.int32, (qb, 1), 0) + i * qb < seq).astype(F32)
            gl[r, :] = (g_ref[r, :].astype(F32) * valid).astype(BF)
            gf[r, :] = jnp.zeros((qb, d), F32)
            ao_ref[r, :] = jnp.zeros((qb, d), F32)
            return c
        lax.fori_loop(0, nb, prep, 0)
        n1t[...] = n1[...].astype(F32).T.astype(BF)
        sq_ref[...] = jnp.zeros_like(sq_ref)

    def project(i, c):
        r = pl.ds(pl.multiple_of(i * qb, qb), qb)
        t = mm(n1[r, :], w3_ref[0]) + b3_ref[0]
        keep = jnp.concatenate([keep_ref[r, :]] * (gw // 128), axis=1)
        up = jnp.concatenate([up_ref[r, :]] * (gw // 128), axis=1)
        down = jnp.concatenate([down_ref[r, :]] * (gw // 128), axis=1)
        for at, ref, scale in ((0, q_s, HEAD_DIM ** -0.5), (1, k_s, None)):
            v = t[:, at * gw:(at + 1) * gw]
            half = ROT // 2
            turned = v * keep + pltpu.roll(v, gw - half, 1) * up + pltpu.roll(v, half, 1) * down
            low = turned.astype(BF)
            ref[r, :] = low if scale is None else (low.astype(F32) * scale).astype(BF)
        v_s[r, :] = t[:, 2 * gw:].astype(BF)
        dc_s[r, :] = mm_rt(gl[r, :], wo_ref[...]).astype(BF)
        for ref in (ctx, dq, dk, dv):
            ref[r, :] = jnp.zeros((qb, gw), F32)
        return c
    lax.fori_loop(0, nb, project, 0)

    key_bias = jnp.where(lax.broadcasted_iota(jnp.int32, (1, rows), 1) < seq, 0.0, MASKED).astype(F32)
    causal = lax.broadcasted_iota(jnp.int32, (qb, qb), 1) <= lax.broadcasted_iota(jnp.int32, (qb, qb), 0)

    def head(h, c):
        lane = lax.broadcasted_iota(jnp.int32, (1, gw), 1) // HEAD_DIM
        mask = jnp.where(lane == h, 1.0, 0.0).astype(F32)
        mask_low = mask.astype(BF)
        for i in range(nb):
            lo, kl = i * qb, (i + 1) * qb
            qm = q_s[lo:kl, :] * mask_low
            dcm = dc_s[lo:kl, :] * mask_low
            s = mm_rt(qm, k_s[:kl, :]) + key_bias[:, :kl]
            diag = jnp.where(causal, s[:, lo:], MASKED)
            s = diag if i == 0 else jnp.concatenate([s[:, :lo], diag], axis=1)
            dp = mm_rt(dcm, v_s[:kl, :])
            e = jnp.exp(s - jnp.max(s, axis=1, keepdims=True))
            p = e * (1.0 / jnp.sum(e, axis=1, keepdims=True))
            p_low = p.astype(BF)
            inner = jnp.sum(p * dp, axis=1, keepdims=True)
            ds = (p * (dp - inner)).astype(BF)
            ctx[lo:kl, :] += mm(p_low, v_s[:kl, :]) * mask
            dq[lo:kl, :] += mm(ds, k_s[:kl, :]) * mask
            dv[:kl, :] += mm_lt(p_low, dcm)
            dk[:kl, :] += mm_lt(ds, qm)
        return c
    lax.fori_loop(0, gw // HEAD_DIM, head, 0)

    def finish(i, c):
        r = pl.ds(pl.multiple_of(i * qb, qb), qb)
        keep = jnp.concatenate([keep_ref[r, :]] * (gw // 128), axis=1)
        up = jnp.concatenate([up_ref[r, :]] * (gw // 128), axis=1)
        down = jnp.concatenate([down_ref[r, :]] * (gw // 128), axis=1)
        half = ROT // 2
        for at, ref, scale in ((0, dq, HEAD_DIM ** -0.5), (1, dk, 1.0)):
            v = ref[r, :] * scale
            turned = v * keep - pltpu.roll(v, gw - half, 1) * up - pltpu.roll(v, half, 1) * down
            d3[r, at * gw:(at + 1) * gw] = turned.astype(BF)
        d3[r, 2 * gw:] = dv[r, :].astype(BF)
        low = ctx[r, :].astype(BF)
        ao_ref[r, :] += mm(low, wo_ref[...])
        gf[r, :] += mm_rt(d3[r, :], w3_ref[0])
        return c
    lax.fori_loop(0, nb, finish, 0)

    dw3 = mm(n1t[...], d3[...])
    dw3_ref[0] = dw3.astype(BF)
    dwo = mm_lt(ctx[...].astype(BF), gl[...])
    dwo_ref[...] = dwo.astype(BF)
    db3 = jnp.sum(d3[...].astype(F32), axis=0, keepdims=True)
    db3_ref[0] = db3
    sq_ref[...] += jnp.sum(dw3 * dw3, axis=0, keepdims=True) + jnp.sum(dwo * dwo, axis=0, keepdims=True) + db3 * db3

    @pl.when(step == last)
    def _():
        def back(i, c):
            r = pl.ds(pl.multiple_of(i * qb, qb), qb)
            normed, inverse = norm_parts(x_ref[r, :].astype(F32))
            e = gf[r, :]
            ff_ref[r, :] = norm_back(e, gain_ref[...], normed, inverse)
            return (c[0] + jnp.sum(e * normed, axis=0, keepdims=True), c[1] + jnp.sum(e, axis=0, keepdims=True))
        zero = jnp.zeros((1, d), F32)
        dgain, dshift = lax.fori_loop(0, nb, back, (zero, zero))
        dgain_ref[...] = dgain
        dshift_ref[...] = dshift
        sq_ref[...] += dgain * dgain + dshift * dshift


def attention(lengths, x, g, gain, shift, w3, b3, wo):
    rows, d = x.shape
    gw = d // GROUPS
    tables = [jnp.asarray(t) for t in rotary_tables(rows, 128)]
    whole = lambda *shape: pl.BlockSpec(shape, lambda j: (0,) * len(shape))
    grid_spec = pl.GridSpec(
        grid=(GROUPS,),
        in_specs=[
            pl.BlockSpec(memory_space=pltpu.SMEM),
            whole(rows, d), whole(rows, d), whole(1, d), whole(1, d),
            pl.BlockSpec((1, d, d), lambda j: (j, 0, 0)),
            pl.BlockSpec((1, 1, d), lambda j: (j, 0, 0)),
            pl.BlockSpec((gw, d), lambda j: (j, 0)),
            whole(rows, 128), whole(rows, 128), whole(rows, 128),
        ],
        out_specs=[
            pl.BlockSpec((1, d, d), lambda j: (j, 0, 0)),
            pl.BlockSpec((gw, d), lambda j: (j, 0)),
            pl.BlockSpec((1, 1, d), lambda j: (j, 0, 0)),
            whole(1, d), whole(1, d), whole(1, d),
            whole(rows, d), whole(rows, d),
        ],
        scratch_shapes=[
            pltpu.VMEM((rows, d), BF), pltpu.VMEM((d, rows), BF), pltpu.VMEM((rows, d), BF), pltpu.VMEM((rows, d), F32),
            pltpu.VMEM((rows, gw), BF), pltpu.VMEM((rows, gw), BF), pltpu.VMEM((rows, gw), BF), pltpu.VMEM((rows, gw), BF),
            pltpu.VMEM((rows, d), BF),
            pltpu.VMEM((rows, gw), F32), pltpu.VMEM((rows, gw), F32), pltpu.VMEM((rows, gw), F32), pltpu.VMEM((rows, gw), F32),
        ],
    )
    flops = 2 * 3 * rows * (d * 3 * d + d * d) + 12 * HEADS * rows * rows * HEAD_DIM
    return pl.pallas_call(
        attn_kernel,
        grid_spec=grid_spec,
        out_shape=[
            jax.ShapeDtypeStruct((GROUPS, d, d), BF),
            jax.ShapeDtypeStruct((d, d), BF),
            jax.ShapeDtypeStruct((GROUPS, 1, d), F32),
            jax.ShapeDtypeStruct((1, d), F32), jax.ShapeDtypeStruct((1, d), F32), jax.ShapeDtypeStruct((1, d), F32),
            jax.ShapeDtypeStruct((rows, d), F32), jax.ShapeDtypeStruct((rows, d), F32),
        ],
        compiler_params=pltpu.CompilerParams(vmem_limit_bytes=VMEM_LIMIT),
        cost_estimate=pl.CostEstimate(flops=flops * 3, bytes_accessed=30_000_000, transcendentals=HEADS * rows * rows),
        name="attention",
    )(lengths, x, g, gain, shift, w3, b3, wo, *tables)


ERF_P = 0.3275911
ERF_A = (0.254829592, -0.284496736, 1.421413741, -1.453152027, 1.061405429)


def gelu_parts(u):
    z = jnp.abs(u) * (2.0 ** -0.5)
    t = 1.0 / (1.0 + ERF_P * z)
    bell = jnp.exp(-0.5 * (u * u))
    a1, a2, a3, a4, a5 = (0.5 * a for a in ERF_A)
    tail = ((((a5 * t + a4) * t + a3) * t + a2) * t + a1) * t * bell
    cdf = jnp.where(u >= 0.0, 1.0 - tail, tail)
    return u * cdf, cdf + u * bell * (1.0 / math.sqrt(2.0 * math.pi))


def ffn_kernel(len_ref, x_ref, g_ref, gain_ref, shift_ref, wu_ref, bu_ref, wd_ref, bias_ref, ao_ref, ff_ref,
               dwu_ref, dwd_ref, dbu_ref, dgain_ref, dshift_ref, dbd_ref, sq_ref, out_ref, gx_ref,
               n2, n2t, gl, gs, act, gup, acc):
    step = pl.program_id(0)
    last = pl.num_programs(0) - 1
    rows, d = x_ref.shape
    fc = wu_ref.shape[2]
    rb = 256
    nb = rows // rb
    seq = len_ref[0]

    @pl.when(step == 0)
    def _():
        def prep(i, c):
            r = pl.ds(pl.multiple_of(i * rb, rb), rb)
            normed, _ = norm_parts(x_ref[r, :].astype(F32))
            low = normed * gain_ref[...] + shift_ref[...]
            n2[r, :] = low.astype(BF)
            valid = (lax.broadcasted_iota(jnp.int32, (rb, 1), 0) + i * rb < seq).astype(F32)
            gl[r, :] = (g_ref[r, :].astype(F32) * valid).astype(BF)
            gs[r, :] = jnp.zeros((rb, d), F32)
            acc[r, :] = jnp.zeros((rb, d), F32)
            return c
        lax.fori_loop(0, nb, prep, 0)
        n2t[...] = n2[...].astype(F32).T.astype(BF)
        sq_ref[...] = jnp.zeros_like(sq_ref)

    def rows_step(i, dbu):
        r = pl.ds(pl.multiple_of(i * rb, rb), rb)
        u = mm(n2[r, :], wu_ref[0]) + bu_ref[0]
        da = mm_rt(gl[r, :], wd_ref[0])
        a, slope = gelu_parts(u)
        a_low = a.astype(BF)
        act[r, :] = a_low
        gu = (da * slope).astype(BF)
        gup[r, :] = gu
        acc[r, :] += mm(a_low, wd_ref[0])
        gs[r, :] += mm_rt(gu, wu_ref[0])
        return dbu + jnp.sum(gu.astype(F32), axis=0, keepdims=True)
    dbu = lax.fori_loop(0, nb, rows_step, jnp.zeros((1, fc), F32))
    dbu_ref[0] = dbu

    dwu = mm(n2t[...], gup[...])
    dwu_ref[0] = dwu.astype(BF)
    dwd = mm_lt(act[...], gl[...])
    dwd_ref[0] = dwd.astype(BF)
    wide = jnp.sum(dwu * dwu, axis=0, keepdims=True) + dbu * dbu
    total = jnp.sum(dwd * dwd, axis=0, keepdims=True)
    sq_ref[:, :d] += total
    sq_ref[:, :fc] += wide

    @pl.when(step == last)
    def _():
        def back(i, c):
            r = pl.ds(pl.multiple_of(i * rb, rb), rb)
            x = x_ref[r, :].astype(F32)
            normed, inverse = norm_parts(x)
            e = gs[r, :]
            grad_rows = gl[r, :].astype(F32)
            gx_ref[r, :] = (grad_rows + ff_ref[r, :] + norm_back(e, gain_ref[...], normed, inverse)).astype(BF)
            valid = (lax.broadcasted_iota(jnp.int32, (rb, 1), 0) + i * rb < seq).astype(F32)
            out_ref[r, :] = ((x + ao_ref[r, :] + acc[r, :] + bias_ref[...]) * valid).astype(BF)
            return (c[0] + jnp.sum(e * normed, axis=0, keepdims=True), c[1] + jnp.sum(e, axis=0, keepdims=True),
                    c[2] + jnp.sum(grad_rows, axis=0, keepdims=True))
        zero = jnp.zeros((1, d), F32)
        dgain, dshift, dbd = lax.fori_loop(0, nb, back, (zero, zero, zero))
        dgain_ref[...] = dgain
        dshift_ref[...] = dshift
        dbd_ref[...] = dbd
        sq_ref[:, :d] += dgain * dgain + dshift * dshift + 2.0 * dbd * dbd


def ffn(lengths, x, g, gain, shift, wu3, bu3, wd3, bias, ao, ff):
    rows, d = x.shape
    chunks, _, fc = wu3.shape
    whole = lambda *shape: pl.BlockSpec(shape, lambda j: (0,) * len(shape))
    grid_spec = pl.GridSpec(
        grid=(chunks,),
        in_specs=[
            pl.BlockSpec(memory_space=pltpu.SMEM),
            whole(rows, d), whole(rows, d), whole(1, d), whole(1, d),
            pl.BlockSpec((1, d, fc), lambda j: (j, 0, 0)),
            pl.BlockSpec((1, 1, fc), lambda j: (j, 0, 0)),
            pl.BlockSpec((1, fc, d), lambda j: (j, 0, 0)),
            whole(1, d), whole(rows, d), whole(rows, d),
        ],
        out_specs=[
            pl.BlockSpec((1, d, fc), lambda j: (j, 0, 0)),
            pl.BlockSpec((1, fc, d), lambda j: (j, 0, 0)),
            pl.BlockSpec((1, 1, fc), lambda j: (j, 0, 0)),
            whole(1, d), whole(1, d), whole(1, d), whole(1, max(d, fc)),
            whole(rows, d), whole(rows, d),
        ],
        scratch_shapes=[
            pltpu.VMEM((rows, d), BF), pltpu.VMEM((d, rows), BF), pltpu.VMEM((rows, d), BF), pltpu.VMEM((rows, d), F32),
            pltpu.VMEM((rows, fc), BF), pltpu.VMEM((rows, fc), BF), pltpu.VMEM((rows, d), F32),
        ],
    )
    return pl.pallas_call(
        ffn_kernel,
        grid_spec=grid_spec,
        out_shape=[
            jax.ShapeDtypeStruct((chunks, d, fc), BF), jax.ShapeDtypeStruct((chunks, fc, d), BF),
            jax.ShapeDtypeStruct((chunks, 1, fc), F32),
            jax.ShapeDtypeStruct((1, d), F32), jax.ShapeDtypeStruct((1, d), F32), jax.ShapeDtypeStruct((1, d), F32),
            jax.ShapeDtypeStruct((1, max(d, fc)), F32),
            jax.ShapeDtypeStruct((rows, d), BF), jax.ShapeDtypeStruct((rows, d), BF),
        ],
        compiler_params=pltpu.CompilerParams(vmem_limit_bytes=VMEM_LIMIT),
        cost_estimate=pl.CostEstimate(flops=2 * 6 * rows * d * fc * chunks * 2, bytes_accessed=40_000_000, transcendentals=rows * fc * chunks),
        name="feedforward",
    )(lengths, x, g, gain, shift, wu3, bu3, wd3, bias, ao, ff)


def xor_permute(value, axis, size, bit):
    return lax.ppermute(value, axis, [(i, i ^ bit) for i in range(size)])


def all_norms(own, sizes):
    rep, fsdp = sizes
    me = lax.axis_index("rep") * fsdp + lax.axis_index("fsdp")
    row = jnp.where(jnp.arange(rep * fsdp) == me, own, 0.0)
    for axis, size in (("fsdp", fsdp), ("rep", rep)):
        if size & (size - 1):
            row = lax.psum(row, axis)
            continue
        bit = 1
        while bit < size:
            row = row + xor_permute(row, axis, size, bit)
            bit *= 2
    return row


def per_device(sizes, block_input, cotangent, lengths, first_gain, first_shift, second_gain, second_shift, triple_weight, triple_bias,
               output_weight, output_bias, upward_weight, upward_bias, downward_weight, downward_bias):
    rep, n = sizes
    rows, d = block_input.shape
    dn = first_gain.shape[0]
    fn = upward_bias.shape[0]
    f = fn * n
    gw = d // GROUPS
    chunks = f // d
    gather = lambda v: lax.all_gather(v, "fsdp", axis=0, tiled=True)

    small = jnp.concatenate([first_gain, first_shift, second_gain, second_shift, output_bias, downward_bias, triple_bias, upward_bias])
    small = gather(small.reshape(1, -1)).astype(F32)
    cut = lambda at, width: small[:, at:at + width].reshape(1, -1)
    gain1, shift1, gain2, shift2, bias_o, bias_d = (cut(i * dn, dn) for i in range(6))
    bias_t = cut(6 * dn, 3 * dn)
    bias_u = cut(9 * dn, fn)
    wt = gather(triple_weight)
    wo = gather(output_weight)
    wu = gather(upward_weight)
    wd = gather(downward_weight)

    by_group = lambda v: jnp.stack([jnp.concatenate([v[:, a * d + j * gw:a * d + (j + 1) * gw] for a in range(3)], axis=1) for j in range(GROUPS)])
    dw3, dwo, db3, dgain1, dshift1, sq1, ao, ff = attention(lengths, block_input, cotangent, gain1, shift1, by_group(wt), by_group(bias_t), wo)
    wu4 = jnp.stack([wu[:, j * d:(j + 1) * d] for j in range(chunks)])
    dwu4, dwd4, dbu, dgain2, dshift2, dbd, sq2, out, gx = ffn(
        lengths, block_input, cotangent, gain2, shift2, wu4, bias_u.reshape(chunks, 1, d), wd.reshape(chunks, d, d), bias_o + bias_d, ao, ff)

    own = jnp.sqrt(jnp.sum(sq1) + jnp.sum(sq2))
    norms = all_norms(own, sizes)
    factor = jnp.minimum(1.0, jnp.mean(norms) / own) / norms.shape[0]

    shards = lambda v: v.reshape(v.shape[0], n, dn, d).swapaxes(0, 1).reshape(n, -1, d)
    ungroup = lambda v: jnp.concatenate([v[:, 0, a * gw:(a + 1) * gw] for a in range(3)], axis=0).reshape(n, 3 * dn)
    vec = lambda v: v.reshape(n, -1)
    smalls = jnp.concatenate([vec(dgain1), vec(dshift1), vec(dgain2), vec(dshift2), vec(dbd), ungroup(db3), vec(dbu)], axis=1)
    small_rows = 8
    smalls = jnp.pad(smalls, ((0, 0), (0, small_rows * d - smalls.shape[1]))).reshape(n, small_rows, d)
    scale = lambda v: (v.astype(F32) * factor).astype(BF)
    pack = jnp.concatenate([scale(shards(dw3)), scale(shards(dwo[None])), scale(shards(dwu4)), scale(dwd4.reshape(n, fn, d)), scale(smalls)], axis=1)
    mine = lax.psum_scatter(pack, "fsdp", scatter_dimension=0, tiled=True)[0]
    mine = lax.psum(mine, "rep").astype(F32)

    at = 0
    def take(count):
        nonlocal at
        at += count
        return mine[at - count:at]
    t3 = take(3 * dn).reshape(GROUPS, dn, d)
    g_triple = jnp.concatenate([t3[j, :, a * gw:(a + 1) * gw] for a in range(3) for j in range(GROUPS)], axis=1)
    g_out = take(dn)
    up = take(chunks * dn).reshape(chunks, dn, d)
    g_up = jnp.concatenate([up[j] for j in range(chunks)], axis=1)
    g_down = take(fn)
    sm = take(small_rows).reshape(-1)
    part = lambda at, width: sm[at:at + width]
    g1, s1, g2, s2, bd = (part(i * dn, dn) for i in range(5))
    return (out, gx, g1, s1, g2, s2, g_triple, part(5 * dn, 3 * dn), g_out, bd, g_up, part(8 * dn, fn), g_down, bd, norms)


def solution(mesh):
    rows = P(("rep", "fsdp"), None)
    vec, mat = P("fsdp"), P("fsdp", None)
    sizes = (mesh.shape["rep"], mesh.shape["fsdp"])
    return jax.shard_map(
        lambda *args: per_device(sizes, *args),
        mesh=mesh,
        in_specs=(rows, rows, P(("rep", "fsdp")), vec, vec, vec, vec, mat, vec, mat, vec, mat, vec, mat, vec),
        out_specs=(rows, rows, vec, vec, vec, vec, mat, vec, mat, vec, mat, vec, mat, vec, P()),
        check_vma=False,
    )
```

time: 1000 us -> 507 us (0.51); the launches traced: 987 us -> 506 us
  matrix products: 283 us -> 0 us
  Pallas kernels: 0 us -> 129 us
  other arithmetic: 134 us -> 25.5 us
  blocking collectives: 121 us -> 31.5 us
  local copies, waits for them, and re-layouts: 109 us -> 43.9 us
  waiting for transfers between devices: 306 us -> 254 us
    dot_general x26 -> x0, matrix products: 283 us -> none  [the longest x4 41.7 us: block_scores(): jnp.einsum('qhd,khd->hqk', query_part, key_low, preferred_element_type=jn...]
    pallas_call x0 -> x2, Pallas kernels: none -> 129 us  [the longest x1 75.7 us: attention(): pl.pallas_call(attn_kernel, grid_spec=grid_spec, out_shape=[jax.ShapeDtyp...]
    reduce_scatter x4 -> x1, waiting for transfers between devices: 243 us -> 144 us  [per_device(): mine = lax.psum_scatter(pack, 'fsdp', scatter_dimension=0, tiled=True)[0]]
    unnamed x3 -> x1, blocking collectives: 97.9 us -> 31.5 us
    dynamic_update_slice x4 -> x0, local copies, waits for them, and re-layouts: 63.4 us -> none  [per_device(): contexts, log_totals = lax.map(attend_forward, jnp.arange(block_count))]
    convert_element_type x26 -> x3, other arithmetic: 61.5 us -> 1.23 us  [per_device(): scale = lambda v: (v.astype(F32) * factor).astype(BF)]
    reduce_sum x14 -> x3, other arithmetic: 37.5 us -> 4.35 us  [the longest x2 2.58 us: per_device(): own = jnp.sqrt(jnp.sum(sq1) + jnp.sum(sq2))]
    all_gather x4, waiting for transfers between devices: 6.33 us -> 37.9 us  [per_device(): gather = lambda v: lax.all_gather(v, 'fsdp', axis=0, tiled=True)]
  transfers between devices with their start and end apart: 9 -> 11, of which waited for: 5 -> 7; matrix products, arithmetic and copies ran while one was open for 45% -> 8% of each run, Pallas kernels for 0% -> 15%
where the time goes in v1:
time: 507 us; the launch traced here: 506 us
  waiting for transfers between devices  254 us (50%)
  Pallas kernels  129 us (25%)
  local copies, waits for them, and re-layouts  43.9 us (9%)
  blocking collectives  31.5 us (6%)
  other arithmetic  25.5 us (5%)
  between operations  17.8 us (4%)
    reduce_scatter x1, waiting for transfers between devices, per_device(): mine = lax.psum_scatter(pack, 'fsdp', scatter_dimension=0, tiled=True)[0]  144 us
    pallas_call x1, Pallas kernels, attention(): pl.pallas_call(attn_kernel, grid_spec=grid_spec, out_shape=[jax.ShapeDtyp...  75.7 us
    psum x1, waiting for transfers between devices, per_device(): mine = lax.psum(mine, 'rep').astype(F32)  66.3 us
    pallas_call x1, Pallas kernels, ffn(): pl.pallas_call(ffn_kernel, grid_spec=grid_spec, out_shape=[jax.ShapeDtype...  53.5 us
    all_gather x4, waiting for transfers between devices, per_device(): gather = lambda v: lax.all_gather(v, 'fsdp', axis=0, tiled=True)  37.9 us
    unnamed x1, blocking collectives  31.5 us
    unnamed x37, local copies, waits for them, and re-layouts  13.2 us
  transfers between devices with their start and end apart: 11, of which 7 were waited for; matrix products, arithmetic and copies ran while one was open for 8% of the time, Pallas kernels for 15%

profile of v1, /device:TPU:0, one launch (start us, length us, event | category | flops | bytes accessed | tf_op | source)
XLA Modules:
  0.0 506.4 jit_solution(3442986648051109880)
XLA Ops:
  10.0 1.2 dynamic-slice
  11.9 5.5 %concatenate.36 = bf16[1248]{0:T(1024)(128)(2,1)S(1)} concatenate(bf16[96]{0:T(256)(128)(2,1)} %param.21, bf16[96]{0:T(256)(128)(2,1)} %param.22, bf16[96]{0:T(256)(128)(2,1)} %param.23, bf16[96]{0:T(256)(128)(2,1)} %param.24, bf16[96]{0:T(256)(128)(2,1)} %param.28, bf16[96]{0:T(256)(128)(2,1)} %param.32, bf16[288]{0:T(512)(128)(2,1)} %param.26, bf16[384]{0:T(512)(128)(2,1)} %param.30), dimensions={0} | concatenate | bytes 4992 | tf_op jit(solution)/shard_map/concatenate | solution.py:379
  17.7 31.5 %all-reduce.1 = bf16[9984]{0:T(1024)(128)(2,1)S(1)} all-reduce(bf16[9984]{0:T(1024)(128)(2,1)S(1)} %dynamic-update-slice), channel_id=2, replica_groups=mesh['rep'=4,'fsdp'=8] {'fsdp'}, use_global_device_ids=true, to_apply=%add.1 | all-reduce | flops 9984 | bytes 39936
  54.8 2.2 fusion.10
  57.3 2.0 pad_maximum_fusion.1.w3_ref
  59.3 18.5 %all-gather.12.cloned.1.call-done.wo_ref = bf16[768,768]{1,0:T(8,128)(2,1)} async-done(((bf16[96,768]{1,0:T(8,128)(2,1)}), bf16[768,768]{1,0:T(8,128)(2,1)}) %all-gather.12.cloned.1.call-update) | async-done | bytes 1179664 | tf_op jit(solution)/shard_map/all_gather | solution.py:377
  77.8 75.7 %attention.1 = (bf16[3,768,768]{2,1,0:T(8,128)(2,1)}, bf16[768,768]{1,0:T(8,128)(2,1)}, f32[3,1,768]{2,1,0:T(1,128)}, f32[1,768]{1,0:T(1,128)}, f32[1,768]{1,0:T...) custom-call(s32[1]{0:T(128)S(6)} %copy.57.len_ref, bf16[1024,768]{1,0:T(8,128)(2,1)} %x_ref.3, ...), custom_call_target="tpu_custom_call" | custom-call | flops 72477573120 | bytes 30000000 | tf_op jit(solution)/shard_map/attention/pallas_call | solution.py:205
  157.1 1.3 reduce_sum.27
  158.4 2.7 slice_bitcast_fusion.3
  161.1 2.5 pad_maximum_fusion.wu_ref
  163.5 19.5 %all-gather.8.cloned.1.call-done = bf16[3072,768]{1,0:T(8,128)(2,1)} async-done(((bf16[384,768]{1,0:T(8,128)(2,1)}), bf16[3072,768]{1,0:T(8,128)(2,1)}) %all-gather.8.cloned.1.call-update) | async-done | bytes 4718608 | tf_op jit(solution)/shard_map/all_gather | solution.py:377
  183.0 53.5 %feedforward.1 = (bf16[4,768,768]{2,1,0:T(8,128)(2,1)}, bf16[4,768,768]{2,1,0:T(8,128)(2,1)}, f32[4,1,768]{2,1,0:T(1,128)}, f32[1,768]{1,0:T(1,128)}, f32[1,768]...) custom-call(s32[1]{0:T(128)S(6)} %copy.57.len_ref, ...), custom_call_target="tpu_custom_call" | custom-call | flops 57982058496 | bytes 40000000 | tf_op jit(solution)/shard_map/feedforward/pallas_call | solution.py:333
  236.5 1.3 reduce_sum.28
  239.9 1.3 reduce.2
  241.2 1.3 reshape.152
  243.6 1.3 reduce.3
  244.9 1.3 reshape.153
  248.6 1.2 collective-permute-start.2
  249.8 1.3 reduce.4
  251.1 1.3 reshape.154
  254.4 1.5 collective-permute-start.3
  255.9 1.3 reduce.5
  259.4 1.5 collective-permute-start.4
  260.8 1.3 reshape.156
  262.1 1.4 concatenate.44
  263.6 1.8 fusion.9
  267.0 2.0 constant_dynamic-update-slice_fusion.3
  269.3 1.5 slice-done.2
  275.6 2.5 constant_dynamic-update-slice_fusion.1
  278.1 2.6 constant_dynamic-update-slice_fusion
  281.4 144.1 %reduce-scatter.2.cloned.1.call-done = bf16[1,1160,768]{2,1,0:T(8,128)(2,1)} async-done(((bf16[8,1160,768]{2,1,0:T(8,128)(2,1)}), bf16[1,1160,768]{2,1,0:T(8,128)(2,1)}) %reduce-scatter.2.cloned.1.call-update) | async-done | bytes 1781776 | tf_op jit(solution)/shard_map/reduce_scatter | solution.py:408
  425.5 66.3 %all-reduce.4.cloned.1.call-done = bf16[1160,768]{1,0:T(8,128)(2,1)} async-done(((bf16[1160,768]{1,0:T(8,128)(2,1)}), bf16[1160,768]{1,0:T(8,128)(2,1)}) %all-reduce.4.cloned.1.call-update) | async-done | bytes 1781776 | tf_op jit(solution)/shard_map/psum | solution.py:409
  (104 shorter events, 34.4 us)
Async XLA Ops:
  7.2 47.7 %all-gather.10.cloned.1.call-start = ((), (), s32[]{:S(2)}) async-start(), calls=%async_computation.3 | async-start | bytes 3981312 | tf_op jit(solution)/shard_map/all_gather | solution.py:377
  7.9 69.9 %all-gather.12.cloned.1.call-start = ((), (), s32[]{:S(2)}) async-start(), calls=%async_computation.4 | async-start | bytes 1327104 | tf_op jit(solution)/shard_map/all_gather | solution.py:377
  8.7 149.7 %all-gather.6.cloned.1.call-start = ((), (), s32[]{:S(2)}) async-start(), calls=%async_computation.1 | async-start | bytes 5308416 | tf_op jit(solution)/shard_map/all_gather | solution.py:377
  9.4 173.6 %all-gather.8.cloned.1.call-start = ((), (), s32[]{:S(2)}) async-start(), calls=%async_computation.2 | async-start | bytes 5308416 | tf_op jit(solution)/shard_map/all_gather | solution.py:377
  10.0 415.5 %reduce-scatter.2.cloned.1.call-start = ((), (), s32[]{:S(2)}) async-start(), calls=%async_computation.5 | async-start | bytes 16035840 | tf_op jit(solution)/shard_map/reduce_scatter | solution.py:408
  183.0 83.0 %copy-start.1 = (bf16[3,768,768]{2,1,0:T(8,128)(2,1)S(1)}, bf16[3,768,768]{2,1,0:T(8,128)(2,1)}, u32[]{:S(2)}) copy-start(bf16[3,768,768]{2,1,0:T(8,128)(2,1)} %get-tuple-element.36) | copy-start | bytes 10616836
  239.7 2.9 collective-permute-start
  243.6 3.8 collective-permute-start.1
  248.6 4.7 collective-permute-start.2
  254.4 3.8 collective-permute-start.3
  259.4 4.2 collective-permute-start.4
  267.0 3.8 slice-start.2
  267.0 2.1 copy-start.2
  267.0 3.9 slice-start.3
  270.9 2.2 slice-start
  271.9 1.5 slice-start.1
  273.4 1.0 copy-start.3
  281.4 210.5 %all-reduce.4.cloned.1.call-start = ((), (), s32[]{:S(2)}) async-start(), calls=%async_computation.6 | async-start | bytes 3563520 | tf_op jit(solution)/shard_map/psum | solution.py:409
  491.9 3.9 copy-start
  493.3 5.7 %copy-start.5 = (f32[96]{0:T(128)}, f32[96]{0:T(128)S(1)}, u32[]{:S(2)}) copy-start(f32[96]{0:T(128)S(1)} %get-tuple-element.122) | copy-start | bytes 1156
  495.8 2.1 copy-start.4
Sparse Core Ops, SparseCore 0:
  9.7 44.8 all-gather.9
  56.2 21.5 all-gather.11
  79.4 51.4 all-gather.5
  132.5 50.4 all-gather.7
  281.5 143.9 reduce-scatter.1
  428.9 62.9 all-reduce.3

commit v2 on v1

v2 whole, which is shorter than its diff:
```python
import math
import numpy as np
import jax
import jax.numpy as jnp
from jax import lax
from jax.experimental import pallas as pl
from jax.experimental.pallas import tpu as pltpu
from jax.sharding import PartitionSpec as P

HEADS = 12
HEAD_DIM = 64
ROT = 16
EPS = 1e-05
MASKED = -1e30
BF = jnp.bfloat16
F32 = jnp.float32
GROUPS = 3
VMEM_LIMIT = 60 * 1024 * 1024


def mm(a, b):
    return jnp.dot(a, b, preferred_element_type=F32)


def mm_rt(a, b):
    return lax.dot_general(a, b, (((1,), (1,)), ((), ())), preferred_element_type=F32)


def mm_lt(a, b):
    return lax.dot_general(a, b, (((0,), (0,)), ((), ())), preferred_element_type=F32)


def rotary_tables(rows, width):
    half = ROT // 2
    freq = np.exp(np.arange(half, dtype=np.float32) * np.float32(-2.0 * math.log(10000.0) / ROT))
    ang = np.arange(rows, dtype=np.float32)[:, None] * freq.astype(np.float32)[None, :]
    cos, sin = np.cos(ang), np.sin(ang)
    keep = np.ones((rows, HEAD_DIM), np.float32)
    up = np.zeros((rows, HEAD_DIM), np.float32)
    down = np.zeros((rows, HEAD_DIM), np.float32)
    keep[:, :half] = cos
    keep[:, half:ROT] = cos
    up[:, :half] = -sin
    down[:, half:ROT] = sin
    rep = width // HEAD_DIM
    return tuple(np.tile(t, (1, rep)).astype(np.float32) for t in (keep, up, down))


def norm_parts(values):
    centred = values - jnp.mean(values, axis=-1, keepdims=True)
    inverse = lax.rsqrt(jnp.mean(centred * centred, axis=-1, keepdims=True) + EPS)
    return centred * inverse, inverse


def norm_back(e, gain, normed, inverse):
    t = e * gain
    t_mean = jnp.mean(t, axis=-1, keepdims=True)
    cross = jnp.mean(t * normed, axis=-1, keepdims=True)
    return inverse * (t - t_mean - normed * cross)


SMALL = 16


def write_halves(value, tmp, keep_ref, send_ref, core, dn, at=None):
    tmp[...] = value.astype(BF)
    for z in range(keep_ref.shape[0]):
        mine = pl.ds(pl.multiple_of((2 * z + core) * dn, 16), dn)
        other = pl.ds(pl.multiple_of((2 * z + 1 - core) * dn, 16), dn)
        keep_ref[z, 0] = tmp[mine, :]
        send_ref[z, 0] = tmp[other, :]


def attn_kernel(split, sc_ref, x_ref, g_ref, par_ref, b3_ref, keep_ref, up_ref, down_ref, *rest):
    nw = split["pieces"]
    w_refs, rest = rest[:nw], rest[nw:]
    nd = 2 if split["on"] else 1
    dw_refs, rest = rest[:nd], rest[nd:]
    sm_ref, ao_ref, ff_ref, rest = rest[0], rest[1], rest[2], rest[3:]
    w, n1, n1t, gl, gf, q_s, k_s, v_s, dc_s, d3, ctx_all, ctx, dq, dk, dv, tmp, sems = rest
    step = pl.program_id(0)
    last = pl.num_programs(0) - 1
    rows, d = x_ref.shape
    gw = d // GROUPS
    qb = 256
    nb = rows // qb
    seq = sc_ref[0]
    gain, shift = par_ref[0:1, :], par_ref[1:2, :]

    def copies():
        if not split["on"]:
            return [pltpu.make_async_copy(w_refs[0].at[m], w.at[m], sems.at[m]) for m in range(GROUPS + 1)]
        z, core, rep = sc_ref[1], sc_ref[2], sc_ref[3]
        dn, nz, nr = split["dn"], split["nz"], split["nr"]
        own, sib, near, sibs = w_refs[0], w_refs[1], w_refs[2:2 + nr], w_refs[2 + nr]
        place = lambda zz, cc: pl.ds(pl.multiple_of((zz * 2 + cc) * dn, 16), dn)
        out = []
        for m in range(nr):
            out.append((own.at[m], w.at[m, place(z, core)], m))
            out.append((sib.at[m], w.at[m, place(z, 1 - core)], m))
        for j in range(nr):
            for k in range(1, nz):
                m, zz = rep ^ j, z ^ k
                out.append((near[j].at[k - 1], w.at[m, place(zz, core)], j))
                out.append((sibs.at[j, k - 1], w.at[m, place(zz, 1 - core)], j))
        return [pltpu.make_async_copy(a, b, sems.at[i]) for i, (a, b, _) in enumerate(out)]

    @pl.when(step == 0)
    def _():
        for c in copies():
            c.start()

        def prep(i, c):
            r = pl.ds(pl.multiple_of(i * qb, qb), qb)
            normed, _ = norm_parts(x_ref[r, :].astype(F32))
            low = normed * gain + shift
            n1[r, :] = low.astype(BF)
            valid = (lax.broadcasted_iota(jnp.int32, (qb, 1), 0) + i * qb < seq).astype(F32)
            gl[r, :] = (g_ref[r, :].astype(F32) * valid).astype(BF)
            gf[r, :] = jnp.zeros((qb, d), F32)
            return c
        lax.fori_loop(0, nb, prep, 0)
        n1t[...] = n1[...].astype(F32).T.astype(BF)
        sm_ref[...] = jnp.zeros_like(sm_ref)
        for c in copies():
            c.wait()

    @pl.when(step < GROUPS)
    def _():
        w3 = w.at[step]
        wo = w.at[GROUPS, pl.ds(pl.multiple_of(step * gw, gw), gw)]

        def project(i, c):
            r = pl.ds(pl.multiple_of(i * qb, qb), qb)
            t = mm(n1[r, :], w3[...]) + b3_ref[0]
            keep = jnp.concatenate([keep_ref[r, :]] * (gw // 128), axis=1)
            up = jnp.concatenate([up_ref[r, :]] * (gw // 128), axis=1)
            down = jnp.concatenate([down_ref[r, :]] * (gw // 128), axis=1)
            half = ROT // 2
            for at, ref, scale in ((0, q_s, HEAD_DIM ** -0.5), (1, k_s, None)):
                v = t[:, at * gw:(at + 1) * gw]
                turned = v * keep + pltpu.roll(v, gw - half, 1) * up + pltpu.roll(v, half, 1) * down
                low = turned.astype(BF)
                ref[r, :] = low if scale is None else (low.astype(F32) * scale).astype(BF)
            v_s[r, :] = t[:, 2 * gw:].astype(BF)
            dc_s[r, :] = mm_rt(gl[r, :], wo[...]).astype(BF)
            for ref in (ctx, dq, dk, dv):
                ref[r, :] = jnp.zeros((qb, gw), F32)
            return c
        lax.fori_loop(0, nb, project, 0)

        key_bias = jnp.where(lax.broadcasted_iota(jnp.int32, (1, rows), 1) < seq, 0.0, MASKED).astype(F32)
        causal = lax.broadcasted_iota(jnp.int32, (qb, qb), 1) <= lax.broadcasted_iota(jnp.int32, (qb, qb), 0)

        def head(h, c):
            lane = lax.broadcasted_iota(jnp.int32, (1, gw), 1) // HEAD_DIM
            mask = jnp.where(lane == h, 1.0, 0.0).astype(F32)
            mask_low = mask.astype(BF)
            for i in range(nb):
                lo, kl = i * qb, (i + 1) * qb
                qm = q_s[lo:kl, :] * mask_low
                dcm = dc_s[lo:kl, :] * mask_low
                s = mm_rt(qm, k_s[:kl, :]) + key_bias[:, :kl]
                diag = jnp.where(causal, s[:, lo:], MASKED)
                s = diag if i == 0 else jnp.concatenate([s[:, :lo], diag], axis=1)
                dp = mm_rt(dcm, v_s[:kl, :])
                e = jnp.exp(s - jnp.max(s, axis=1, keepdims=True))
                p = e * (1.0 / jnp.sum(e, axis=1, keepdims=True))
                p_low = p.astype(BF)
                inner = jnp.sum(p * dp, axis=1, keepdims=True)
                ds = (p * (dp - inner)).astype(BF)
                ctx[lo:kl, :] += mm(p_low, v_s[:kl, :]) * mask
                dq[lo:kl, :] += mm(ds, k_s[:kl, :]) * mask
                dv[:kl, :] += mm_lt(p_low, dcm)
                dk[:kl, :] += mm_lt(ds, qm)
            return c
        lax.fori_loop(0, gw // HEAD_DIM, head, 0)

        def finish(i, c):
            r = pl.ds(pl.multiple_of(i * qb, qb), qb)
            keep = jnp.concatenate([keep_ref[r, :]] * (gw // 128), axis=1)
            up = jnp.concatenate([up_ref[r, :]] * (gw // 128), axis=1)
            down = jnp.concatenate([down_ref[r, :]] * (gw // 128), axis=1)
            half = ROT // 2
            for at, ref, scale in ((0, dq, HEAD_DIM ** -0.5), (1, dk, 1.0)):
                v = ref[r, :] * scale
                turned = v * keep - pltpu.roll(v, gw - half, 1) * up - pltpu.roll(v, half, 1) * down
                d3[r, at * gw:(at + 1) * gw] = turned.astype(BF)
            d3[r, 2 * gw:] = dv[r, :].astype(BF)
            ctx_all[r, pl.ds(pl.multiple_of(step * gw, gw), gw)] = ctx[r, :].astype(BF)
            gf[r, :] += mm_rt(d3[r, :], w3[...])
            return c
        lax.fori_loop(0, nb, finish, 0)
        db3 = jnp.sum(d3[...].astype(F32), axis=0, keepdims=True)
        sm_ref[pl.ds(2 + step, 1), :] = db3
        sm_ref[5:6, :] += db3 * db3

    def store(dw):
        sm_ref[5:6, :] += jnp.sum(dw * dw, axis=0, keepdims=True)
        if split["on"]:
            write_halves(dw, tmp, dw_refs[0], dw_refs[1], sc_ref[2], split["dn"])
        else:
            dw_refs[0][0] = dw.astype(BF)

    @pl.when(step < GROUPS)
    def _():
        store(mm(n1t[...], d3[...]))

    @pl.when(step == last)
    def _():
        store(mm_lt(ctx_all[...], gl[...]))

        def back(i, c):
            r = pl.ds(pl.multiple_of(i * qb, qb), qb)
            ao_ref[r, :] = mm(ctx_all[r, :], w[GROUPS])
            normed, inverse = norm_parts(x_ref[r, :].astype(F32))
            e = gf[r, :]
            ff_ref[r, :] = norm_back(e, gain, normed, inverse)
            return (c[0] + jnp.sum(e * normed, axis=0, keepdims=True), c[1] + jnp.sum(e, axis=0, keepdims=True))
        zero = jnp.zeros((1, d), F32)
        dgain, dshift = lax.fori_loop(0, nb, back, (zero, zero))
        sm_ref[0:1, :] = dgain
        sm_ref[1:2, :] = dshift
        sm_ref[5:6, :] += dgain * dgain + dshift * dshift


def attention(split, scalars, x, g, par, b3, weights):
    rows, d = x.shape
    gw = d // GROUPS
    tables = [jnp.asarray(t) for t in rotary_tables(rows, 128)]
    whole = lambda *shape: pl.BlockSpec(shape, lambda j: (0,) * len(shape))
    any_ = pl.BlockSpec(memory_space=pl.ANY)
    split = dict(split, pieces=len(weights))
    if split["on"]:
        nz, dn = split["nz"], split["dn"]
        dw_specs = [pl.BlockSpec((nz, 1, dn, d), lambda j: (0, j, 0, 0))] * 2
        dw_shapes = [jax.ShapeDtypeStruct((nz, GROUPS + 1, dn, d), BF)] * 2
    else:
        dw_specs = [pl.BlockSpec((1, d, d), lambda j: (j, 0, 0))]
        dw_shapes = [jax.ShapeDtypeStruct((GROUPS + 1, d, d), BF)]
    grid_spec = pl.GridSpec(
        grid=(GROUPS + 1,),
        in_specs=[
            pl.BlockSpec(memory_space=pltpu.SMEM),
            whole(rows, d), whole(rows, d), whole(*par.shape),
            pl.BlockSpec((1, 1, d), lambda j: (jnp.minimum(j, GROUPS - 1), 0, 0)),
            whole(rows, 128), whole(rows, 128), whole(rows, 128),
        ] + [any_] * len(weights),
        out_specs=dw_specs + [whole(8, d), whole(rows, d), whole(rows, d)],
        scratch_shapes=[
            pltpu.VMEM((GROUPS + 1, d, d), BF),
            pltpu.VMEM((rows, d), BF), pltpu.VMEM((d, rows), BF), pltpu.VMEM((rows, d), BF), pltpu.VMEM((rows, d), F32),
            pltpu.VMEM((rows, gw), BF), pltpu.VMEM((rows, gw), BF), pltpu.VMEM((rows, gw), BF), pltpu.VMEM((rows, gw), BF),
            pltpu.VMEM((rows, d), BF), pltpu.VMEM((rows, d), BF),
            pltpu.VMEM((rows, gw), F32), pltpu.VMEM((rows, gw), F32), pltpu.VMEM((rows, gw), F32), pltpu.VMEM((rows, gw), F32),
            pltpu.VMEM((d, d), BF), pltpu.SemaphoreType.DMA((64,)),
        ],
    )
    flops = 2 * 3 * rows * (d * 3 * d + d * d) + 12 * HEADS * rows * rows * HEAD_DIM
    return pl.pallas_call(
        lambda *refs: attn_kernel(split, *refs),
        grid_spec=grid_spec,
        out_shape=dw_shapes + [
            jax.ShapeDtypeStruct((8, d), F32),
            jax.ShapeDtypeStruct((rows, d), F32), jax.ShapeDtypeStruct((rows, d), F32),
        ],
        compiler_params=pltpu.CompilerParams(vmem_limit_bytes=VMEM_LIMIT),
        cost_estimate=pl.CostEstimate(flops=flops * 3, bytes_accessed=30_000_000, transcendentals=HEADS * rows * rows),
        name="attention",
    )(scalars, x, g, par, b3, *tables, *weights)


ERF_P = 0.3275911
ERF_A = (0.254829592, -0.284496736, 1.421413741, -1.453152027, 1.061405429)


def gelu_parts(u):
    z = jnp.abs(u) * (2.0 ** -0.5)
    t = 1.0 / (1.0 + ERF_P * z)
    bell = jnp.exp(-0.5 * (u * u))
    a1, a2, a3, a4, a5 = (0.5 * a for a in ERF_A)
    tail = ((((a5 * t + a4) * t + a3) * t + a2) * t + a1) * t * bell
    cdf = jnp.where(u >= 0.0, 1.0 - tail, tail)
    return u * cdf, cdf + u * bell * (1.0 / math.sqrt(2.0 * math.pi))


def ffn_kernel(split, sc_ref, x_ref, g_ref, par_ref, wu_ref, bu_ref, wd_ref, ao_ref, ff_ref, sm1_ref, *rest):
    nd = 4 if split["on"] else 2
    dw_refs, rest = rest[:nd], rest[nd:]
    sm_ref, norm_ref, out_ref, gx_ref = rest[:4]
    n2, n2t, gl, gs, act, gup, acc, sq, tmp = rest[4:]
    step = pl.program_id(0)
    last = pl.num_programs(0) - 1
    rows, d = x_ref.shape
    fc = wu_ref.shape[1]
    rb = 256
    nb = rows // rb
    seq = sc_ref[0]
    gain, shift = par_ref[2:3, :], par_ref[3:4, :]

    @pl.when(step == 0)
    def _():
        def prep(i, c):
            r = pl.ds(pl.multiple_of(i * rb, rb), rb)
            normed, _ = norm_parts(x_ref[r, :].astype(F32))
            low = normed * gain + shift
            n2[r, :] = low.astype(BF)
            valid = (lax.broadcasted_iota(jnp.int32, (rb, 1), 0) + i * rb < seq).astype(F32)
            gl[r, :] = (g_ref[r, :].astype(F32) * valid).astype(BF)
            gs[r, :] = jnp.zeros((rb, d), F32)
            acc[r, :] = jnp.zeros((rb, d), F32)
            return c
        lax.fori_loop(0, nb, prep, 0)
        n2t[...] = n2[...].astype(F32).T.astype(BF)
        sq[...] = jnp.zeros_like(sq)
        sm_ref[...] = jnp.zeros_like(sm_ref)

    def rows_step(i, dbu):
        r = pl.ds(pl.multiple_of(i * rb, rb), rb)
        u = mm(n2[r, :], wu_ref[...]) + bu_ref[0]
        da = mm_rt(gl[r, :], wd_ref[...])
        a, slope = gelu_parts(u)
        a_low = a.astype(BF)
        act[r, :] = a_low
        gu = (da * slope).astype(BF)
        gup[r, :] = gu
        acc[r, :] += mm(a_low, wd_ref[...])
        gs[r, :] += mm_rt(gu, wu_ref[...])
        return dbu + jnp.sum(gu.astype(F32), axis=0, keepdims=True)
    dbu = lax.fori_loop(0, nb, rows_step, jnp.zeros((1, fc), F32))
    sm_ref[pl.ds(8 + step, 1), :] = dbu

    dwu = mm(n2t[...], gup[...])
    total = jnp.sum(dwu * dwu, axis=0, keepdims=True) + dbu * dbu
    if split["on"]:
        write_halves(dwu, tmp, dw_refs[0], dw_refs[1], sc_ref[2], split["dn"])
    else:
        dw_refs[0][0] = dwu.astype(BF)
    dwd = mm_lt(act[...], gl[...])
    total += jnp.sum(dwd * dwd, axis=0, keepdims=True)
    if split["on"]:
        tmp[...] = dwd.astype(BF)
        core, dn, nr = sc_ref[2], split["dn"], split["nr"]
        for m in range(nr):
            dw_refs[2][0, m] = tmp[pl.ds(pl.multiple_of((core * nr + m) * dn, 16), dn), :]
            dw_refs[3][0, m] = tmp[pl.ds(pl.multiple_of(((1 - core) * nr + m) * dn, 16), dn), :]
    else:
        dw_refs[1][0] = dwd.astype(BF)
    sq[...] += total

    @pl.when(step == last)
    def _():
        def back(i, c):
            r = pl.ds(pl.multiple_of(i * rb, rb), rb)
            x = x_ref[r, :].astype(F32)
            normed, inverse = norm_parts(x)
            e = gs[r, :]
            grad_rows = gl[r, :].astype(F32)
            gx_ref[r, :] = (grad_rows + ff_ref[r, :] + norm_back(e, gain, normed, inverse)).astype(BF)
            valid = (lax.broadcasted_iota(jnp.int32, (rb, 1), 0) + i * rb < seq).astype(F32)
            bias = par_ref[4:5, :] + par_ref[5:6, :]
            out_ref[r, :] = ((x + ao_ref[r, :] + acc[r, :] + bias) * valid).astype(BF)
            return (c[0] + jnp.sum(e * normed, axis=0, keepdims=True), c[1] + jnp.sum(e, axis=0, keepdims=True),
                    c[2] + jnp.sum(grad_rows, axis=0, keepdims=True))
        zero = jnp.zeros((1, d), F32)
        dgain, dshift, dbd = lax.fori_loop(0, nb, back, (zero, zero, zero))
        sm_ref[0:2, :] = sm1_ref[0:2, :]
        sm_ref[2:3, :] = dgain
        sm_ref[3:4, :] = dshift
        sm_ref[4:5, :] = dbd
        sm_ref[5:8, :] = sm1_ref[2:5, :]
        final = sq[...] + sm1_ref[5:6, :] + dgain * dgain + dshift * dshift + 2.0 * dbd * dbd
        own = jnp.sqrt(jnp.sum(final, axis=1, keepdims=True))
        here = lax.broadcasted_iota(jnp.int32, norm_ref.shape, 1) == sc_ref[4]
        norm_ref[...] = jnp.where(here, own, 0.0)


def ffn(split, scalars, x, g, par, wu, bu, wd, ao, ff, sm1, norm_width):
    rows, d = x.shape
    chunks = wu.shape[1] // d
    fc = d
    whole = lambda *shape: pl.BlockSpec(shape, lambda j: (0,) * len(shape))
    if split["on"]:
        nz, dn, nr = split["nz"], split["dn"], split["nr"]
        dw_specs = [pl.BlockSpec((nz, 1, dn, d), lambda j: (0, j, 0, 0))] * 2 + [pl.BlockSpec((1, nr, dn, d), lambda j: (j, 0, 0, 0))] * 2
        dw_shapes = [jax.ShapeDtypeStruct((nz, chunks, dn, d), BF)] * 2 + [jax.ShapeDtypeStruct((nz, nr, dn, d), BF)] * 2
    else:
        dw_specs = [pl.BlockSpec((1, d, fc), lambda j: (j, 0, 0)), pl.BlockSpec((1, fc, d), lambda j: (j, 0, 0))]
        dw_shapes = [jax.ShapeDtypeStruct((chunks, d, fc), BF), jax.ShapeDtypeStruct((chunks, fc, d), BF)]
    grid_spec = pl.GridSpec(
        grid=(chunks,),
        in_specs=[
            pl.BlockSpec(memory_space=pltpu.SMEM),
            whole(rows, d), whole(rows, d), whole(*par.shape),
            pl.BlockSpec((d, fc), lambda j: (0, j)),
            pl.BlockSpec((1, 1, fc), lambda j: (j, 0, 0)),
            pl.BlockSpec((fc, d), lambda j: (j, 0)),
            whole(rows, d), whole(rows, d), whole(8, d),
        ],
        out_specs=dw_specs + [whole(SMALL, d), whole(1, norm_width), whole(rows, d), whole(rows, d)],
        scratch_shapes=[
            pltpu.VMEM((rows, d), BF), pltpu.VMEM((d, rows), BF), pltpu.VMEM((rows, d), BF), pltpu.VMEM((rows, d), F32),
            pltpu.VMEM((rows, fc), BF), pltpu.VMEM((rows, fc), BF), pltpu.VMEM((rows, d), F32), pltpu.VMEM((1, d), F32),
            pltpu.VMEM((d, d), BF),
        ],
    )
    return pl.pallas_call(
        lambda *refs: ffn_kernel(split, *refs),
        grid_spec=grid_spec,
        out_shape=dw_shapes + [
            jax.ShapeDtypeStruct((SMALL, d), F32), jax.ShapeDtypeStruct((1, norm_width), F32),
            jax.ShapeDtypeStruct((rows, d), BF), jax.ShapeDtypeStruct((rows, d), BF),
        ],
        compiler_params=pltpu.CompilerParams(vmem_limit_bytes=VMEM_LIMIT),
        cost_estimate=pl.CostEstimate(flops=2 * 6 * rows * d * fc * chunks * 2, bytes_accessed=40_000_000, transcendentals=rows * fc * chunks),
        name="feedforward",
    )(scalars, x, g, par, wu, bu, wd, ao, ff, sm1)


def xor_permute(value, axis, size, bit):
    return lax.ppermute(value, axis, [(i, i ^ bit) for i in range(size)])


def butterfly(value, axis, size):
    if size & (size - 1):
        return lax.psum(value, axis)
    bit = 1
    while bit < size:
        value = value + xor_permute(value, axis, size, bit)
        bit *= 2
    return value


def per_device(sizes, block_input, cotangent, lengths, first_gain, first_shift, second_gain, second_shift, triple_weight, triple_bias,
               output_weight, output_bias, upward_weight, upward_bias, downward_weight, downward_bias):
    rep, n = sizes
    rows, d = block_input.shape
    dn, fn = first_gain.shape[0], upward_bias.shape[0]
    gw = d // GROUPS
    chunks = fn * n // d
    nz = n // 2
    split = dict(on=rep == 4 and n == 8 and dn % 16 == 0 and chunks == nz == rep, dn=dn, nz=nz, nr=rep)
    ri, fi = lax.axis_index("rep"), lax.axis_index("fsdp")
    z, core = fi // 2, fi % 2
    scalars = jnp.stack([lengths[0], z, core, ri, ri * n + fi]).astype(jnp.int32)
    gather = lambda v: lax.all_gather(v, "fsdp", axis=0, tiled=True)
    group_cols = lambda v, j: jnp.concatenate([v[:, a * d + j * gw:a * d + (j + 1) * gw] for a in range(3)], axis=1)
    mats = jnp.stack([group_cols(triple_weight, j) for j in range(GROUPS)] + [output_weight])

    small = jnp.concatenate([first_gain, first_shift, second_gain, second_shift, output_bias, downward_bias, triple_bias, upward_bias])
    small = jnp.where(jnp.arange(n)[:, None] == fi, small[None], 0.0).astype(BF)

    if split["on"]:
        quarter = lax.dynamic_index_in_dim(mats, ri, 0, keepdims=False)
        far = jnp.stack([xor_permute(quarter, "fsdp", n, 2 * k) for k in range(1, nz)])
        sib_own = xor_permute(mats, "fsdp", n, 1)
        small = butterfly(small, "fsdp", n)
        near = [far] + [xor_permute(far, "rep", rep, j) for j in range(1, rep)]
        sibs = xor_permute(jnp.stack(near), "fsdp", n, 1)
        weights = [mats, sib_own] + near + [sibs]
        late_up, late_down, _ = lax.optimization_barrier((upward_weight, downward_weight, far[0, 0, 0]))
        wu, wd = gather(late_up), gather(late_down)
    else:
        small = butterfly(small, "fsdp", n)
        weights = [lax.all_gather(mats, "fsdp", axis=1, tiled=True)]
        wu, wd = gather(upward_weight), gather(downward_weight)

    small = small.astype(F32)
    par = small[:, :6 * dn].reshape(n, 6, dn).swapaxes(0, 1).reshape(6, d)
    par = jnp.pad(par, ((0, 2), (0, 0)))
    bias_t = small[:, 6 * dn:9 * dn].reshape(1, 3 * d)
    b3 = jnp.stack([group_cols(bias_t, j) for j in range(GROUPS)])
    bu = small[:, 9 * dn:].reshape(chunks, 1, d)

    *dwa, sm1, ao, ff = attention(split, scalars, block_input, cotangent, par, b3, weights)
    width = -(-rep * n // 128) * 128
    *dwf, smalls, norm_row, out, gx = ffn(split, scalars, block_input, cotangent, par, wu, bu, wd, ao, ff, sm1, width)

    norm_row = butterfly(butterfly(norm_row, "fsdp", n), "rep", rep)
    norms = norm_row[0, :rep * n]
    mean = jnp.mean(norms)
    factor_of = lambda at: jnp.minimum(1.0, mean / lax.dynamic_index_in_dim(norms, at, 0, keepdims=False)) / (rep * n)
    me = ri * n + fi
    factor = factor_of(me)

    if split["on"]:
        other = factor_of(me ^ 1)
        zh, zl, y, x = z // 2, z % 2, ri // 2, ri % 2
        places = dict(x=(3, x, "rep", rep, 1), y=(2, y, "rep", rep, 2), lo=(1, zl, "fsdp", n, 2), hi=(0, zh, "fsdp", n, 4))

        def hop(held, name):
            axis, bit, mesh_axis, size, flip = places[name]
            send = lax.dynamic_slice_in_dim(held, 1 - bit, 1, axis)
            got = xor_permute(send, mesh_axis, size, flip)
            keep = lax.dynamic_slice_in_dim(held, bit, 1, axis)
            return (keep.astype(F32) + got.astype(F32)).astype(BF)

        def paired(keep, send):
            got = xor_permute(send, "fsdp", n, 1)
            both = keep.astype(F32) * factor + got.astype(F32) * other
            return both.astype(BF).reshape(2, 2, 2, 2, dn, d)

        smalls = smalls * factor + xor_permute(smalls, "fsdp", n, 1) * other
        smalls = jnp.broadcast_to(smalls.astype(BF), (2, 2, 2, 2, SMALL, d))
        part_a = paired(dwa[0], dwa[1])
        part_u = paired(dwf[0], dwf[1])
        part_d = jnp.concatenate([paired(dwf[2], dwf[3]), smalls], axis=4)
        for name in ("x", "y", "lo"):
            part_a = hop(part_a, name)
        for name in ("y", "lo", "x"):
            part_u = hop(part_u, name)
        for name in ("lo", "x", "y"):
            part_d = hop(part_d, name)
        mine = hop(jnp.concatenate([part_a, part_u, part_d], axis=4), "hi").reshape(3 * dn + SMALL, d)
        smalls = mine[3 * dn:].astype(F32)
        mine = mine[:3 * dn]
        around = [mine] + [xor_permute(mine, "rep", rep, j) for j in range(1, rep)]
        flip = lambda bit, a, b: (jnp.where(bit == 1, b, a), jnp.where(bit == 1, a, b))
        a0, a1 = flip(x, around[0], around[1])
        a2, a3 = flip(x, around[2], around[3])
        a0, a2 = flip(y, a0, a2)
        a1, a3 = flip(y, a1, a3)
        final = jnp.stack([a0, a1, a2, a3]).astype(F32)
        g_att, g_up, g_down = final[:, :dn], final[:, dn:2 * dn], final[:, 2 * dn:].reshape(fn, d)
        smalls = smalls.reshape(SMALL, d)
    else:
        scale = lambda v: (v.astype(F32) * factor).astype(BF)
        shards = lambda v: v.reshape(v.shape[0], n, dn, d).swapaxes(0, 1).reshape(n, -1, d)
        pack = jnp.concatenate([scale(shards(dwa[0])), scale(shards(dwf[0])), scale(dwf[1].reshape(n, fn, d))], axis=1)
        mine = lax.psum_scatter(pack, "fsdp", scatter_dimension=0, tiled=True)[0]
        mine = lax.psum(mine, "rep").astype(F32)
        g_att = mine[:4 * dn].reshape(4, dn, d)
        g_up = mine[4 * dn:(4 + chunks) * dn].reshape(chunks, dn, d)
        g_down = mine[(4 + chunks) * dn:]
        smalls = lax.psum(scale(smalls), ("rep", "fsdp")).astype(F32)

    g_triple = jnp.concatenate([g_att[j, :, a * gw:(a + 1) * gw] for a in range(3) for j in range(GROUPS)], axis=1)
    g_upward = jnp.concatenate([g_up[j] for j in range(chunks)], axis=1)
    own = lambda v, width: lax.dynamic_slice_in_dim(v, fi * width, width, 0)
    g1, s1, g2, s2, bd = (own(smalls[i], dn) for i in range(5))
    b_triple = own(jnp.concatenate([smalls[5 + j, a * gw:(a + 1) * gw] for a in range(3) for j in range(GROUPS)]), 3 * dn)
    b_up = own(smalls[8:8 + chunks].reshape(-1), fn)
    return (out, gx, g1, s1, g2, s2, g_triple, b_triple, g_att[GROUPS], bd, g_upward, b_up, g_down, bd, norms)


def solution(mesh):
    rows = P(("rep", "fsdp"), None)
    vec, mat = P("fsdp"), P("fsdp", None)
    sizes = (mesh.shape["rep"], mesh.shape["fsdp"])
    return jax.shard_map(
        lambda *args: per_device(sizes, *args),
        mesh=mesh,
        in_specs=(rows, rows, P(("rep", "fsdp")), vec, vec, vec, vec, mat, vec, mat, vec, mat, vec, mat, vec),
        out_specs=(rows, rows, vec, vec, vec, vec, mat, vec, mat, vec, mat, vec, mat, vec, P()),
        check_vma=False,
    )
```

time: 507 us -> 349 us (0.69)
  waiting for transfers between devices: 254 us -> 109 us
  starting transfers between devices: 4.63 us -> 56.2 us
  blocking collectives: 31.5 us -> 0 us
  local copies, waits for them, and re-layouts: 43.9 us -> 12.9 us
    reduce_scatter x1 -> x0, waiting for transfers between devices: 144 us -> none  [per_device(): mine = lax.psum_scatter(pack, 'fsdp', scatter_dimension=0, tiled=True)[0]]
    ppermute x5 -> x33, waiting for transfers between devices: 2.96 us -> 108 us  [xor_permute(): return lax.ppermute(value, axis, [(i, i ^ bit) for i in range(size)])]
    psum x1 -> x0, waiting for transfers between devices: 66.3 us -> none  [per_device(): mine = lax.psum(mine, 'rep').astype(F32)]
    ppermute x5 -> x33, starting transfers between devices: 4.4 us -> 56.1 us  [xor_permute(): return lax.ppermute(value, axis, [(i, i ^ bit) for i in range(size)])]
    all_gather x4 -> x2, waiting for transfers between devices: 37.9 us -> 0.04 us  [per_device(): gather = lambda v: lax.all_gather(v, 'fsdp', axis=0, tiled=True)]
    unnamed x1 -> x0, blocking collectives: 31.5 us -> none
    convert_element_type x3 -> x17, other arithmetic: 1.23 us -> 14.7 us  [the longest x3 7.58 us: paired(): return both.astype(BF).reshape(2, 2, 2, 2, dn, d)]
    unnamed x37 -> x57, local copies, waits for them, and re-layouts: 13.2 us -> 2.6 us
  transfers between devices with their start and end apart: 11 -> 35, of which waited for: 7 -> 21; matrix products, arithmetic and copies ran while one was open for 8% -> 8% of each run, Pallas kernels for 15% -> 38%
where the time goes in v2:
time: 349 us; the launch traced here: 348 us
  Pallas kernels  131 us (38%)
  waiting for transfers between devices  109 us (31%)
  starting transfers between devices  56.2 us (16%)
  other arithmetic  21.3 us (6%)
  between operations  17.5 us (5%)
  local copies, waits for them, and re-layouts  12.9 us (4%)
    ppermute x33, waiting for transfers between devices, xor_permute(): return lax.ppermute(value, axis, [(i, i ^ bit) for i in range(size)])  108 us
    pallas_call x1, Pallas kernels, attention(): pl.pallas_call(lambda *refs: attn_kernel(split, *refs), grid_spec=grid_sp...  77.3 us
    ppermute x33, starting transfers between devices, xor_permute(): return lax.ppermute(value, axis, [(i, i ^ bit) for i in range(size)])  56.1 us
    pallas_call x1, Pallas kernels, ffn(): pl.pallas_call(lambda *refs: ffn_kernel(split, *refs), grid_spec=grid_spe...  54.2 us
    convert_element_type x3, other arithmetic, paired(): return both.astype(BF).reshape(2, 2, 2, 2, dn, d)  7.58 us
  transfers between devices with their start and end apart: 35, of which 21 were waited for; matrix products, arithmetic and copies ran while one was open for 8% of the time, Pallas kernels for 38%

profile of v2, /device:TPU:0, one launch (start us, length us, event | category | flops | bytes accessed | tf_op | source)
XLA Modules:
  0.0 348.4 jit_solution(10935138643954767231)
XLA Ops:
  9.3 3.1 collective-permute-start.4
  12.4 2.6 collective-permute-start.5
  15.1 3.1 collective-permute-done.4
  18.2 12.8 %collective-permute-done.5 = bf16[96,768]{1,0:T(8,128)(2,1)S(1)} collective-permute-done((bf16[96,768]{1,0:T(8,128)(2,1)S(1)}, bf16[96,768]{1,0:T(8,128)(2,1)S(1)}, u32[]{:S(2)}, u32[]{:S(2)}) %collective-permute-start.5) | collective-permute-done | bytes 147488 | tf_op jit(solution)/shard_map/ppermute | solution.py:421
  34.7 6.0 %collective-permute-done.7.refs_11_ = bf16[3,96,768]{2,1,0:T(8,128)(2,1)S(1)} collective-permute-done((bf16[3,96,768]{2,1,0:T(8,128)(2,1)S(1)}, bf16[3,96,768]{2,1,0:T(8,128)(2,1)S(1)}, u32[]{:S(2)}, u32[]{:S(2)}) %collective-permute-start.7) | collective-permute-done | bytes 442400 | tf_op jit(solution)/shard_map/ppermute | solution.py:421
  40.7 5.9 %collective-permute-done.8.refs_12_ = bf16[3,96,768]{2,1,0:T(8,128)(2,1)S(1)} collective-permute-done((bf16[3,96,768]{2,1,0:T(8,128)(2,1)S(1)}, bf16[3,96,768]{2,1,0:T(8,128)(2,1)S(1)}, u32[]{:S(2)}, u32[]{:S(2)}) %collective-permute-start.8) | collective-permute-done | bytes 442400 | tf_op jit(solution)/shard_map/ppermute | solution.py:421
  47.6 12.4 %collective-permute-start.1 = (bf16[8,1248]{1,0:T(8,128)(2,1)S(1)}, bf16[8,1248]{1,0:T(8,128)(2,1)S(1)}, u32[]{:S(2)}, u32[]{:S(2)}) collective-permute-start(bf16[8,1248]{1,0:T(8,128)(2,1)S(1)} %fusion.13), channel_id=1, source_target_pairs={{0,2},{1,3},{2,0},{3,1},{4,6},{5,7},{6,4},{7,5},{8,10},{9,11},{10,... | collective-permute-start | bytes 59912 | tf_op jit(solution)/shard_map/ppermute | solution.py:421
  61.8 5.4 %collective-permute-start.2 = (bf16[8,1248]{1,0:T(8,128)(2,1)S(1)}, bf16[8,1248]{1,0:T(8,128)(2,1)S(1)}, u32[]{:S(2)}, u32[]{:S(2)}) collective-permute-start(bf16[8,1248]{1,0:T(8,128)(2,1)S(1)} %fusion.24), channel_id=1, source_target_pairs={{0,4},{1,5},{2,6},{3,7},{4,0},{5,1},{6,2},{7,3},{8,12},{9,13},{10,... | collective-permute-start | bytes 59912 | tf_op jit(solution)/shard_map/ppermute | solution.py:421
  72.1 77.3 %attention.1 = (bf16[4,4,96,768]{3,2,1,0:T(8,128)(2,1)}, bf16[4,4,96,768]{3,2,1,0:T(8,128)(2,1)}, f32[8,768]{1,0:T(8,128)}, f32[1024,768]{1,0:T(8,128)}, f32[1024,768]{1,0:T(8,128)}) custom-call(s32[5]{0:T(128)} %stack.88.refs_0_, bf16[1024,768]{1,0:T(8,128)(2,1)} %refs_1_.3, bf16[1024,768]{1,0:T(8,128)(2,1)} %refs_2_.3, f32[8,768]{1,0:T(8,128)} %pad.4.refs_3_, ...), custom_call_target="tpu_custom_call" | custom-call | flops 72477573120 | bytes 30000000 | tf_op jit(solution)/shard_map/attention/pallas_call | solution.py:260
  149.5 54.2 %feedforward.1 = (bf16[4,4,96,768]{3,2,1,0:T(8,128)(2,1)}, bf16[4,4,96,768]{3,2,1,0:T(8,128)(2,1)}, bf16[4,4,96,768]{3,2,1,0:T(8,128)(2,1)}, bf16[4,4,96,768]{3,...) custom-call(s32[5]{0:T(128)} %stack.88.refs_0_, ...), custom_call_target="tpu_custom_call" | custom-call | flops 57982058496 | bytes 40000000 | tf_op jit(solution)/shard_map/feedforward/pallas_call | solution.py:407
  204.7 3.8 %collective-permute-done.11 = f32[1,128]{1,0:T(1,128)S(1)} collective-permute-done((f32[1,128]{1,0:T(1,128)}, f32[1,128]{1,0:T(1,128)S(1)}, u32[]{:S(2)}, u32[]{:S(2)}) %collective-permute-start.11) | collective-permute-done | bytes 544 | tf_op jit(solution)/shard_map/ppermute | solution.py:421
  209.1 2.6 collective-permute-start.12
  213.3 2.9 collective-permute-start.13
  219.2 2.1 collective-permute-done.14
  222.8 2.0 collective-permute-done.15
  228.6 2.5 add_convert_fusion.2
  234.0 2.5 add_convert_fusion.1
  239.5 2.5 add_convert_fusion
  245.4 13.5 %collective-permute-done.17 = bf16[2,2,2,1,96,768]{5,4,3,2,1,0:T(8,128)(2,1)} collective-permute-done((bf16[2,2,2,1,96,768]{5,4,3,2,1,0:T(8,128)(2,1)}, bf16[2,2,2,1,96,768]{5,4,3,2,1,0:T(8,128)(2,1)}, u32[]{:S(2)}, u32[]{:S(2)}) %collective-permute-start.17) | collective-permute-done | bytes 1179680 | tf_op jit(solution)/shard_map/ppermute | solution.py:421
  261.4 5.5 %collective-permute-done.21 = bf16[2,2,1,2,96,768]{5,4,3,2,1,0:T(8,128)(2,1)} collective-permute-done((bf16[2,2,1,2,96,768]{5,4,3,2,1,0:T(8,128)(2,1)}, bf16[2,2,1,2,96,768]{5,4,3,2,1,0:T(8,128)(2,1)}, u32[]{:S(2)}, u32[]{:S(2)}) %collective-permute-start.21) | collective-permute-done | bytes 1179680 | tf_op jit(solution)/shard_map/ppermute | solution.py:421
  268.6 2.1 collective-permute-start.22
  270.7 6.1 %collective-permute-done.26 = bf16[2,1,2,2,112,768]{5,4,3,2,1,0:T(8,128)(2,1)} collective-permute-done((bf16[2,1,2,2,112,768]{5,4,3,2,1,0:T(8,128)(2,1)}, bf16[2,1,2,2,112,768]{5,4,3,2,1,0:T(8,128)(2,1)}, u32[]{:S(2)}, u32[]{:S(2)}) %collective-permute-start.26) | collective-permute-done | bytes 1376288 | tf_op jit(solution)/shard_map/ppermute | solution.py:421
  280.2 2.1 collective-permute-start.19
  282.3 7.0 %collective-permute-done.22 = bf16[2,1,1,2,96,768]{5,4,3,2,1,0:T(8,128)(2,1)S(1)} collective-permute-done((bf16[2,1,1,2,96,768]{5,4,3,2,1,0:T(8,128)(2,1)S(1)}, bf16[2,1,1,2,96,768]{5,4,3,2,1,0:T(8,128)(2,1)S(1)}, u32[]{:S(2)}, u32[]{:S(2)}) %collective-permute-start.22) | collective-permute-done | bytes 589856 | tf_op jit(solution)/shard_map/ppermute | solution.py:421
  291.0 3.6 %collective-permute-done.27 = bf16[2,1,2,1,112,768]{5,4,3,2,1,0:T(8,128)(2,1)S(1)} collective-permute-done((bf16[2,1,2,1,112,768]{5,4,3,2,1,0:T(8,128)(2,1)S(1)}, bf16[2,1,2,1,112,768]{5,4,3,2,1,0:T(8,128)(2,1)S(1)}, u32[]{:S(2)}, u32[]{:S(2)}) %collective-permute-start.27) | collective-permute-done | bytes 688160 | tf_op jit(solution)/shard_map/ppermute | solution.py:421
  295.0 2.8 collective-permute-done.23
  297.9 4.3 %collective-permute-done.28 = bf16[2,1,1,1,112,768]{5,4,3,2,1,0:T(8,128)(2,1)S(1)} collective-permute-done((bf16[2,1,1,1,112,768]{5,4,3,2,1,0:T(8,128)(2,1)S(1)}, bf16[2,1,1,1,112,768]{5,4,3,2,1,0:T(8,128)(2,1)S(1)}, u32[]{:S(2)}, u32[]{:S(2)}) %collective-permute-start.28) | collective-permute-done | bytes 344096 | tf_op jit(solution)/shard_map/ppermute | solution.py:421
  302.4 3.0 collective-permute-start.29
  305.3 13.0 %collective-permute-done.29 = bf16[1,1,1,1,304,768]{5,4,3,2,1,0:T(8,128)(2,1)S(1)} collective-permute-done((bf16[1,1,1,1,304,768]{5,4,3,2,1,0:T(8,128)(2,1)S(1)}, bf16[1,1,1,1,304,768]{5,4,3,2,1,0:T(8,128)(2,1)S(1)}, u32[]{:S(2)}, u32[]{:S(2)}) %collective-permute-start.29) | collective-permute-done | bytes 466976 | tf_op jit(solution)/shard_map/ppermute | solution.py:421
  319.0 2.6 collective-permute-start.31
  326.0 6.6 %collective-permute-done.30 = bf16[288,768]{1,0:T(8,128)(2,1)S(1)} collective-permute-done((bf16[288,768]{1,0:T(8,128)(2,1)S(1)}, bf16[288,768]{1,0:T(8,128)(2,1)S(1)}, u32[]{:S(2)}, u32[]{:S(2)}) %collective-permute-start.30) | collective-permute-done | bytes 442400 | tf_op jit(solution)/shard_map/ppermute | solution.py:421
  332.6 4.9 %collective-permute-done.31 = bf16[288,768]{1,0:T(8,128)(2,1)S(1)} collective-permute-done((bf16[288,768]{1,0:T(8,128)(2,1)S(1)}, bf16[288,768]{1,0:T(8,128)(2,1)S(1)}, u32[]{:S(2)}, u32[]{:S(2)}) %collective-permute-start.31) | collective-permute-done | bytes 442400 | tf_op jit(solution)/shard_map/ppermute | solution.py:421
  (188 shorter events, 50.2 us)
Async XLA Ops:
  7.3 142.2 %all-gather.3.cloned.1.call-start = ((), (), s32[]{:S(2)}) async-start(), calls=%async_computation | async-start | bytes 5308416 | tf_op jit(solution)/shard_map/all_gather | solution.py:446
  8.0 141.5 %all-gather.5.cloned.1.call-start = ((), (), s32[]{:S(2)}) async-start(), calls=%async_computation.1 | async-start | bytes 5308416 | tf_op jit(solution)/shard_map/all_gather | solution.py:446
  9.3 8.9 %collective-permute-start.4 = (bf16[96,768]{1,0:T(8,128)(2,1)S(1)}, bf16[96,768]{1,0:T(8,128)(2,1)S(1)}, u32[]{:S(2)}, u32[]{:S(2)}) collective-permute-start(bf16[96,768]{1,0:T(8,128)(2,1)S(1)} %dynamic-slice_bitcast_fusion), channel_id=1, source_target_pairs={{0,2},{1,3},{2,0},{3,1},{4,6},{5,7},{6,4},{7,5},{8,10},{9,11},{10,... | collective-permute-start | bytes 442376 | tf_op jit(solution)/shard_map/ppermute | solution.py:421
  12.4 18.6 %collective-permute-start.5 = (bf16[96,768]{1,0:T(8,128)(2,1)S(1)}, bf16[96,768]{1,0:T(8,128)(2,1)S(1)}, u32[]{:S(2)}, u32[]{:S(2)}) collective-permute-start(bf16[96,768]{1,0:T(8,128)(2,1)S(1)} %dynamic-slice_bitcast_fusion), channel_id=1, source_target_pairs={{0,4},{1,5},{2,6},{3,7},{4,0},{5,1},{6,2},{7,3},{8,12},{9,13},{10,... | collective-permute-start | bytes 442376 | tf_op jit(solution)/shard_map/ppermute | solution.py:421
  15.0 16.0 %collective-permute-start.6 = (bf16[96,768]{1,0:T(8,128)(2,1)S(1)}, bf16[96,768]{1,0:T(8,128)(2,1)S(1)}, u32[]{:S(2)}, u32[]{:S(2)}) collective-permute-start(bf16[96,768]{1,0:T(8,128)(2,1)S(1)} %dynamic-slice_bitcast_fusion), channel_id=1, source_target_pairs={{0,6},{1,7},{2,4},{3,5},{4,2},{5,3},{6,0},{7,1},{8,14},{9,15},{10,... | collective-permute-start | bytes 442376 | tf_op jit(solution)/shard_map/ppermute | solution.py:421
  31.1 9.7 %collective-permute-start.7 = (bf16[3,96,768]{2,1,0:T(8,128)(2,1)S(1)}, bf16[3,96,768]{2,1,0:T(8,128)(2,1)S(1)}, u32[]{:S(2)}, u32[]{:S(2)}) collective-permute-start(bf16[3,96,768]{2,1,0:T(8,128)(2,1)S(1)} %get-tuple-element.56.refs_10_), channel_id=1, source_target_pairs={{0,8},{8,0},{16,24},{24,16},{1,9},{9,1},{17,25},{25,17},{2,10},{10... | collective-permute-start | bytes 1327112 | tf_op jit(solution)/shard_map/ppermute | solution.py:421
  32.6 14.0 %collective-permute-start.8 = (bf16[3,96,768]{2,1,0:T(8,128)(2,1)S(1)}, bf16[3,96,768]{2,1,0:T(8,128)(2,1)S(1)}, u32[]{:S(2)}, u32[]{:S(2)}) collective-permute-start(bf16[3,96,768]{2,1,0:T(8,128)(2,1)S(1)} %get-tuple-element.56.refs_10_), channel_id=1, source_target_pairs={{0,16},{8,24},{16,0},{24,8},{1,17},{9,25},{17,1},{25,9},{2,18},{10... | collective-permute-start | bytes 1327112 | tf_op jit(solution)/shard_map/ppermute | solution.py:421
  34.1 12.5 %collective-permute-start.9 = (bf16[3,96,768]{2,1,0:T(8,128)(2,1)S(1)}, bf16[3,96,768]{2,1,0:T(8,128)(2,1)S(1)}, u32[]{:S(2)}, u32[]{:S(2)}) collective-permute-start(bf16[3,96,768]{2,1,0:T(8,128)(2,1)S(1)} %get-tuple-element.56.refs_10_), channel_id=1, source_target_pairs={{0,24},{8,16},{16,8},{24,0},{1,25},{9,17},{17,9},{25,1},{2,26},{10... | collective-permute-start | bytes 1327112 | tf_op jit(solution)/shard_map/ppermute | solution.py:421
  34.7 12.8 %collective-permute-start = (bf16[8,1248]{1,0:T(8,128)(2,1)S(1)}, bf16[8,1248]{1,0:T(8,128)(2,1)S(1)}, u32[]{:S(2)}, u32[]{:S(2)}) collective-permute-start(bf16[8,1248]{1,0:T(8,128)(2,1)S(1)} %broadcast_select_fusion.4), channel_id=1, source_target_pairs={{0,1},{1,0},{2,3},{3,2},{4,5},{5,4},{6,7},{7,6},{8,9},{9,8},{10,11... | collective-permute-start | bytes 59912 | tf_op jit(solution)/shard_map/ppermute | solution.py:421
  46.9 24.3 %collective-permute-start.10 = (bf16[4,3,96,768]{3,2,1,0:T(8,128)(2,1)S(1)}, bf16[4,3,96,768]{3,2,1,0:T(8,128)(2,1)}, u32[]{:S(2)}, u32[]{:S(2)}) collective-permute-start(bf16[4,3,96,768]{3,2,1,0:T(8,128)(2,1)S(1)} %pad_maximum_fusion), channel_id=1, source_target_pairs={{0,1},{1,0},{2,3},{3,2},{4,5},{5,4},{6,7},{7,6},{8,9},{9,8},{10,11... | collective-permute-start | bytes 5308424 | tf_op jit(solution)/shard_map/ppermute | solution.py:421
  47.6 14.1 %collective-permute-start.1 = (bf16[8,1248]{1,0:T(8,128)(2,1)S(1)}, bf16[8,1248]{1,0:T(8,128)(2,1)S(1)}, u32[]{:S(2)}, u32[]{:S(2)}) collective-permute-start(bf16[8,1248]{1,0:T(8,128)(2,1)S(1)} %fusion.13), channel_id=1, source_target_pairs={{0,2},{1,3},{2,0},{3,1},{4,6},{5,7},{6,4},{7,5},{8,10},{9,11},{10,... | collective-permute-start | bytes 59912 | tf_op jit(solution)/shard_map/ppermute | solution.py:421
  61.8 7.2 %collective-permute-start.2 = (bf16[8,1248]{1,0:T(8,128)(2,1)S(1)}, bf16[8,1248]{1,0:T(8,128)(2,1)S(1)}, u32[]{:S(2)}, u32[]{:S(2)}) collective-permute-start(bf16[8,1248]{1,0:T(8,128)(2,1)S(1)} %fusion.24), channel_id=1, source_target_pairs={{0,4},{1,5},{2,6},{3,7},{4,0},{5,1},{6,2},{7,3},{8,12},{9,13},{10,... | collective-permute-start | bytes 59912 | tf_op jit(solution)/shard_map/ppermute | solution.py:421
  149.3 79.2 %collective-permute-start.16 = (bf16[4,4,96,768]{3,2,1,0:T(8,128)(2,1)}, bf16[4,4,96,768]{3,2,1,0:T(8,128)(2,1)}, u32[]{:S(2)}, u32[]{:S(2)}) collective-permute-start(bf16[4,4,96,768]{3,2,1,0:T(8,128)(2,1)} %get-tuple-element.39), channel_id=1, source_target_pairs={{0,1},{1,0},{2,3},{3,2},{4,5},{5,4},{6,7},{7,6},{8,9},{9,8},{10,11... | collective-permute-start | bytes 7077896 | tf_op jit(solution)/shard_map/ppermute | solution.py:421
  203.7 30.0 %collective-permute-start.20 = (bf16[4,4,96,768]{3,2,1,0:T(8,128)(2,1)}, bf16[4,4,96,768]{3,2,1,0:T(8,128)(2,1)}, u32[]{:S(2)}, u32[]{:S(2)}) collective-permute-start(bf16[4,4,96,768]{3,2,1,0:T(8,128)(2,1)} %get-tuple-element.41), channel_id=1, source_target_pairs={{0,1},{1,0},{2,3},{3,2},{4,5},{5,4},{6,7},{7,6},{8,9},{9,8},{10,11... | collective-permute-start | bytes 7077896 | tf_op jit(solution)/shard_map/ppermute | solution.py:421
  204.2 35.0 %collective-permute-start.24 = (bf16[4,4,96,768]{3,2,1,0:T(8,128)(2,1)}, bf16[4,4,96,768]{3,2,1,0:T(8,128)(2,1)}, u32[]{:S(2)}, u32[]{:S(2)}) collective-permute-start(bf16[4,4,96,768]{3,2,1,0:T(8,128)(2,1)} %get-tuple-element.43), channel_id=1, source_target_pairs={{0,1},{1,0},{2,3},{3,2},{4,5},{5,4},{6,7},{7,6},{8,9},{9,8},{10,11... | collective-permute-start | bytes 7077896 | tf_op jit(solution)/shard_map/ppermute | solution.py:421
  204.3 4.2 %collective-permute-start.11 = (f32[1,128]{1,0:T(1,128)}, f32[1,128]{1,0:T(1,128)S(1)}, u32[]{:S(2)}, u32[]{:S(2)}) collective-permute-start(f32[1,128]{1,0:T(1,128)} %get-tuple-element.38), channel_id=1, source_target_pairs={{0,1},{1,0},{2,3},{3,2},{4,5},{5,4},{6,7},{7,6},{8,9},{9,8},{10,11... | collective-permute-start | bytes 1544 | tf_op jit(solution)/shard_map/ppermute | solution.py:421
  209.1 4.1 %collective-permute-start.12 = (f32[1,128]{1,0:T(1,128)S(1)}, f32[1,128]{1,0:T(1,128)S(1)}, u32[]{:S(2)}, u32[]{:S(2)}) collective-permute-start(f32[1,128]{1,0:T(1,128)S(1)} %add.155), channel_id=1, source_target_pairs={{0,2},{1,3},{2,0},{3,1},{4,6},{5,7},{6,4},{7,5},{8,10},{9,11},{10,... | collective-permute-start | bytes 1544 | tf_op jit(solution)/shard_map/ppermute | solution.py:421
  213.3 4.4 %collective-permute-start.13 = (f32[1,128]{1,0:T(1,128)S(1)}, f32[1,128]{1,0:T(1,128)S(1)}, u32[]{:S(2)}, u32[]{:S(2)}) collective-permute-start(f32[1,128]{1,0:T(1,128)S(1)} %add.156), channel_id=1, source_target_pairs={{0,4},{1,5},{2,6},{3,7},{4,0},{5,1},{6,2},{7,3},{8,12},{9,13},{10,... | collective-permute-start | bytes 1544 | tf_op jit(solution)/shard_map/ppermute | solution.py:421
  222.8 10.9 %collective-permute-start.25 = (f32[16,768]{1,0:T(8,128)}, f32[16,768]{1,0:T(8,128)S(1)}, u32[]{:S(2)}, u32[]{:S(2)}) collective-permute-start(f32[16,768]{1,0:T(8,128)} %get-tuple-element.44), channel_id=1, source_target_pairs={{0,1},{1,0},{2,3},{3,2},{4,5},{5,4},{6,7},{7,6},{8,9},{9,8},{10,11... | collective-permute-start | bytes 147464 | tf_op jit(solution)/shard_map/ppermute | solution.py:421
  232.2 26.7 %collective-permute-start.17 = (bf16[2,2,2,1,96,768]{5,4,3,2,1,0:T(8,128)(2,1)}, bf16[2,2,2,1,96,768]{5,4,3,2,1,0:T(8,128)(2,1)}, u32[]{:S(2)}, u32[]{:S(2)}) collective-permute-start(bf16[2,2,2,1,96,768]{5,4,3,2,1,0:T(8,128)(2,1)} %constant_dynamic-slice_fusion.13), channel_id=1, source_target_pairs={{0,8},{8,0},{16,24},{24,16},{1,9},{9,1},{17,25},{25,17},{2,10},{10... | collective-permute-start | bytes 3538952 | tf_op jit(solution)/shard_map/ppermute | solution.py:421
  237.7 29.2 %collective-permute-start.21 = (bf16[2,2,1,2,96,768]{5,4,3,2,1,0:T(8,128)(2,1)}, bf16[2,2,1,2,96,768]{5,4,3,2,1,0:T(8,128)(2,1)}, u32[]{:S(2)}, u32[]{:S(2)}) collective-permute-start(bf16[2,2,1,2,96,768]{5,4,3,2,1,0:T(8,128)(2,1)} %constant_dynamic-slice_fusion.10), channel_id=1, source_target_pairs={{0,16},{8,24},{16,0},{24,8},{1,17},{9,25},{17,1},{25,9},{2,18},{10... | collective-permute-start | bytes 3538952 | tf_op jit(solution)/shard_map/ppermute | solution.py:421
  243.3 33.4 %collective-permute-start.26 = (bf16[2,1,2,2,112,768]{5,4,3,2,1,0:T(8,128)(2,1)}, bf16[2,1,2,2,112,768]{5,4,3,2,1,0:T(8,128)(2,1)}, u32[]{:S(2)}, u32[]{:S(2)}) collective-permute-start(bf16[2,1,2,2,112,768]{5,4,3,2,1,0:T(8,128)(2,1)} %fusion), channel_id=1, source_target_pairs={{0,2},{1,3},{2,0},{3,1},{4,6},{5,7},{6,4},{7,5},{8,10},{9,11},{10,... | collective-permute-start | bytes 4128776 | tf_op jit(solution)/shard_map/ppermute | solution.py:421
  260.8 19.2 %collective-permute-start.18 = (bf16[2,2,1,1,96,768]{5,4,3,2,1,0:T(8,128)(2,1)S(1)}, bf16[2,2,1,1,96,768]{5,4,3,2,1,0:T(8,128)(2,1)S(1)}, u32[]{:S(2)}, u32[]{:S(2)}) collective-permute-start(bf16[2,2,1,1,96,768]{5,4,3,2,1,0:T(8,128)(2,1)S(1)} %constant_dynamic-slice_fusion.12), channel_id=1, source_target_pairs={{0,16},{8,24},{16,0},{24,8},{1,17},{9,25},{17,1},{25,9},{2,18},{10... | collective-permute-start | bytes 1769480 | tf_op jit(solution)/shard_map/ppermute | solution.py:421
  268.6 20.7 %collective-permute-start.22 = (bf16[2,1,1,2,96,768]{5,4,3,2,1,0:T(8,128)(2,1)S(1)}, bf16[2,1,1,2,96,768]{5,4,3,2,1,0:T(8,128)(2,1)S(1)}, u32[]{:S(2)}, u32[]{:S(2)}) collective-permute-start(bf16[2,1,1,2,96,768]{5,4,3,2,1,0:T(8,128)(2,1)S(1)} %constant_dynamic-slice_fusion.9), channel_id=1, source_target_pairs={{0,2},{1,3},{2,0},{3,1},{4,6},{5,7},{6,4},{7,5},{8,10},{9,11},{10,... | collective-permute-start | bytes 1769480 | tf_op jit(solution)/shard_map/ppermute | solution.py:421
  278.5 16.1 %collective-permute-start.27 = (bf16[2,1,2,1,112,768]{5,4,3,2,1,0:T(8,128)(2,1)S(1)}, bf16[2,1,2,1,112,768]{5,4,3,2,1,0:T(8,128)(2,1)S(1)}, u32[]{:S(2)}, u32[]{:S(2)}) collective-permute-start(bf16[2,1,2,1,112,768]{5,4,3,2,1,0:T(8,128)(2,1)S(1)} %constant_dynamic-slice_fusion.7), channel_id=1, source_target_pairs={{0,8},{8,0},{16,24},{24,16},{1,9},{9,1},{17,25},{25,17},{2,10},{10... | collective-permute-start | bytes 2064392 | tf_op jit(solution)/shard_map/ppermute | solution.py:421
  280.2 14.7 %collective-permute-start.19 = (bf16[2,1,1,1,96,768]{5,4,3,2,1,0:T(8,128)(2,1)S(1)}, bf16[2,1,1,1,96,768]{5,4,3,2,1,0:T(8,128)(2,1)S(1)}, u32[]{:S(2)}, u32[]{:S(2)}) collective-permute-start(bf16[2,1,1,1,96,768]{5,4,3,2,1,0:T(8,128)(2,1)S(1)} %constant_dynamic-slice_fusion.11), channel_id=1, source_target_pairs={{0,2},{1,3},{2,0},{3,1},{4,6},{5,7},{6,4},{7,5},{8,10},{9,11},{10,... | collective-permute-start | bytes 884744 | tf_op jit(solution)/shard_map/ppermute | solution.py:421
  289.5 8.3 %collective-permute-start.23 = (bf16[2,1,1,1,96,768]{5,4,3,2,1,0:T(8,128)(2,1)S(1)}, bf16[2,1,1,1,96,768]{5,4,3,2,1,0:T(8,128)(2,1)S(1)}, u32[]{:S(2)}, u32[]{:S(2)}) collective-permute-start(bf16[2,1,1,1,96,768]{5,4,3,2,1,0:T(8,128)(2,1)S(1)} %constant_dynamic-slice_fusion.8), channel_id=1, source_target_pairs={{0,8},{8,0},{16,24},{24,16},{1,9},{9,1},{17,25},{25,17},{2,10},{10... | collective-permute-start | bytes 884744 | tf_op jit(solution)/shard_map/ppermute | solution.py:421
  294.8 7.3 %collective-permute-start.28 = (bf16[2,1,1,1,112,768]{5,4,3,2,1,0:T(8,128)(2,1)S(1)}, bf16[2,1,1,1,112,768]{5,4,3,2,1,0:T(8,128)(2,1)S(1)}, u32[]{:S(2)}, u32[]{:S(2)}) collective-permute-start(bf16[2,1,1,1,112,768]{5,4,3,2,1,0:T(8,128)(2,1)S(1)} %constant_dynamic-slice_fusion.6), channel_id=1, source_target_pairs={{0,16},{8,24},{16,0},{24,8},{1,17},{9,25},{17,1},{25,9},{2,18},{10... | collective-permute-start | bytes 1032200 | tf_op jit(solution)/shard_map/ppermute | solution.py:421
  302.4 16.0 %collective-permute-start.29 = (bf16[1,1,1,1,304,768]{5,4,3,2,1,0:T(8,128)(2,1)S(1)}, bf16[1,1,1,1,304,768]{5,4,3,2,1,0:T(8,128)(2,1)S(1)}, u32[]{:S(2)}, u32[]{:S(2)}) collective-permute-start(bf16[1,1,1,1,304,768]{5,4,3,2,1,0:T(8,128)(2,1)S(1)} %constant_dynamic-slice_fusion.5), channel_id=1, source_target_pairs={{0,4},{1,5},{2,6},{3,7},{4,0},{5,1},{6,2},{7,3},{8,12},{9,13},{10,... | collective-permute-start | bytes 1400840 | tf_op jit(solution)/shard_map/ppermute | solution.py:421
  318.5 14.1 %collective-permute-start.30 = (bf16[288,768]{1,0:T(8,128)(2,1)S(1)}, bf16[288,768]{1,0:T(8,128)(2,1)S(1)}, u32[]{:S(2)}, u32[]{:S(2)}) collective-permute-start(bf16[288,768]{1,0:T(8,128)(2,1)S(1)} %slice_bitcast_fusion), channel_id=1, source_target_pairs={{0,24},{8,16},{16,8},{24,0},{1,25},{9,17},{17,9},{25,1},{2,26},{10... | collective-permute-start | bytes 1327112 | tf_op jit(solution)/shard_map/ppermute | solution.py:421
  319.0 18.5 %collective-permute-start.31 = (bf16[288,768]{1,0:T(8,128)(2,1)S(1)}, bf16[288,768]{1,0:T(8,128)(2,1)S(1)}, u32[]{:S(2)}, u32[]{:S(2)}) collective-permute-start(bf16[288,768]{1,0:T(8,128)(2,1)S(1)} %slice_bitcast_fusion), channel_id=1, source_target_pairs={{0,16},{8,24},{16,0},{24,8},{1,17},{9,25},{17,1},{25,9},{2,18},{10... | collective-permute-start | bytes 1327112 | tf_op jit(solution)/shard_map/ppermute | solution.py:421
  321.6 16.0 %collective-permute-start.32 = (bf16[288,768]{1,0:T(8,128)(2,1)S(1)}, bf16[288,768]{1,0:T(8,128)(2,1)S(1)}, u32[]{:S(2)}, u32[]{:S(2)}) collective-permute-start(bf16[288,768]{1,0:T(8,128)(2,1)S(1)} %slice_bitcast_fusion), channel_id=1, source_target_pairs={{0,8},{8,0},{16,24},{24,16},{1,9},{9,1},{17,25},{25,17},{2,10},{10... | collective-permute-start | bytes 1327112 | tf_op jit(solution)/shard_map/ppermute | solution.py:421
  (27 other events, 326.2 us)
Sparse Core Ops, SparseCore 0:
  9.7 58.2 all-gather.2
  69.7 51.5 all-gather.4
